TPU v7x, 128 devices: a whole 4x4x4 slice. The times are simulated.
128 devices in a mesh: ctx: 2 (over core), expert: 64 (over z, x, y).
Axes of the slice: x: 4, y: 4, z: 4, core: 2. Of those that a mesh axis runs over, the one named last changes fastest.
Arguments:
- tokens: bfloat16 [64, 256, 2048], P('expert', 'ctx'), may hold values from -6 to 6
- positions: int32 [64, 256], P('expert'), may hold values from 0 to 191, as said below
- routes: int32 [64, 256, 8], P('expert', 'ctx'), may hold values from 0 to 127, all different within a row; in each aligned block of 128 rows (0 to 127, 128 to 255, ..., all dimensions but the last counted through in order) at most 8 rows name the same one
- attn_gain: bfloat16 [2048], P(('ctx', 'expert')), may hold values from 0.5 to 1.5
- w_query: bfloat16 [2048, 4096], P(('ctx', 'expert')), may hold values from -0.125 to 0.125
- w_key: bfloat16 [2048, 512], P(('ctx', 'expert')), may hold values from -0.125 to 0.125
- w_value: bfloat16 [2048, 512], P(('ctx', 'expert')), may hold values from -0.125 to 0.125
- query_gain: bfloat16 [128], P(('ctx', 'expert')), may hold values from 0.099609375 to 1.8984375
- key_gain: bfloat16 [128], P(('ctx', 'expert')), may hold values from 0.099609375 to 1.8984375
- w_out: bfloat16 [4096, 2048], P(('ctx', 'expert')), may hold values from -0.375 to 0.375
- ffn_gain: bfloat16 [2048], P(('ctx', 'expert')), may hold values from 0.5 to 1.5
- w_router: bfloat16 [2048, 128], P(('ctx', 'expert')), may hold values from -0.0625 to 0.0625
- w_gate: bfloat16 [128, 2048, 768], P(('ctx', 'expert')), may hold values from -0.125 to 0.125
- w_up: bfloat16 [128, 2048, 768], P(('ctx', 'expert')), may hold values from -0.125 to 0.125
- w_down: bfloat16 [128, 768, 2048], P(('ctx', 'expert')), may hold values from -0.875 to 0.875
- cotangent: bfloat16 [64, 256, 2048], P('expert', 'ctx'), may hold values from -6 to 6
Outputs:
- block_out: float32 [64, 256, 2048], P('expert', 'ctx')
- d_tokens: float32 [64, 256, 2048], P('expert', 'ctx')
- d_attn_gain: float32 [2048], P(('ctx', 'expert'))
- d_w_query: float32 [2048, 4096], P(('ctx', 'expert'))
- d_w_key: float32 [2048, 512], P(('ctx', 'expert'))
- d_w_value: float32 [2048, 512], P(('ctx', 'expert'))
- d_query_gain: float32 [128], P(('ctx', 'expert'))
- d_key_gain: float32 [128], P(('ctx', 'expert'))
- d_w_out: float32 [4096, 2048], P(('ctx', 'expert'))
- d_ffn_gain: float32 [2048], P(('ctx', 'expert'))
- d_w_router: float32 [2048, 128], P(('ctx', 'expert'))
- d_w_gate: float32 [128, 2048, 768], P(('ctx', 'expert'))
- d_w_up: float32 [128, 2048, 768], P(('ctx', 'expert'))
- d_w_down: float32 [128, 768, 2048], P(('ctx', 'expert'))
Inputs may be any that keep to these rules, and one draw needn't show every extreme that they name: `positions`: each sequence packs 3 documents end to end; a position is 0 at a document's first token and rises by one a token within it. One document of each sequence holds 192 tokens. `routes`: A token names 8 different experts; the tokens of one device name every expert exactly 8 times.
All inputs are finite; a program needn't handle non-finite values.
Results may differ from a plain program's by a relative error of at most 0.04.
Values may be sent and summed in bfloat16 or wider, within the bound.
No kernel may reach another device: no remote copies, remote signals or barrier semaphores. Data moves between devices by JAX's collectives and lax.ppermute only.
A program may use at most 256 MiB of HBM per device.

v0:
```python
from functools import partial
import math

import jax
import jax.numpy as jnp
from jax import lax
from jax.sharding import PartitionSpec as P

D = 2048
HEADS = 32
KV = 4
HD = 128
FF = 768
TOP = 8
TOK_DEV = 128


epsilon = 1e-06
rope_base = 1000000.0
masked_score = -1e30
highest = lax.Precision.HIGHEST


def in_one_piece(arrays, axis, dim, along):
    widths = [a.shape[along] for a in arrays]
    both = jnp.concatenate(arrays, axis=along)
    out = lax.all_gather(both, axis, axis=dim, tiled=True)
    return tuple(jnp.split(out, [sum(widths[:k]) for k in range(1, len(widths))], axis=along))


def side_by_side(arrays, axis, dim, along):
    columns = [a.reshape(*a.shape[:along], -1) for a in arrays]
    both = jnp.concatenate(columns, axis=along)
    out, at, done = (lax.all_gather(both, axis, axis=dim, tiled=True), 0, [])
    for a, column in zip(arrays, columns):
        slab = out[..., at : at + column.shape[along]]
        done.append(slab.reshape(*slab.shape[:along], *a.shape[along:]))
        at += column.shape[along]
    return tuple(done)


def grouped_exchange(x, axis, split_dim, concat_dim, work, item_dim, out_dim):

    def moved(group):
        return lax.all_to_all(group, axis, split_axis=split_dim, concat_axis=concat_dim, tiled=True)

    items = jax.tree.leaves(x)[0].shape[item_dim]
    ends = [items * k // 2 for k in range(2 + 1)] if items % 2 == 0 else [0, items]
    groups = [
        jax.tree.map(lambda a: lax.slice_in_dim(a, low, high, axis=item_dim), x)
        for low, high in zip(ends, ends[1:])
    ]
    arrived = [moved(group) for group in groups]
    made = [work(group) for group in arrived]
    return jax.tree.map(lambda *parts: jnp.concatenate(parts, axis=out_dim), *made)


def cut_along(x, dim, size):
    shape = x.shape
    pieces = x.reshape(*shape[:dim], size, shape[dim] // size, *shape[dim + 1 :])
    return jnp.moveaxis(pieces, dim, 0)


def sum_at_owner(x, axis, dim):
    size = lax.axis_size(axis)
    pieces = lax.all_to_all(cut_along(x, dim, size), axis, 0, 0, tiled=True)
    return jnp.sum(pieces.astype(jnp.float32), axis=0)


def sent_together(arrays, axis, dim, along):
    widths = [a.shape[along] for a in arrays]
    both = jnp.concatenate(arrays, axis=along)
    out = sum_at_owner(both, axis, dim)
    return tuple(jnp.split(out, [sum(widths[:k]) for k in range(1, len(widths))], axis=along))


def side_by_side_2(arrays, axis, dim, along):
    widths = [a.shape[along] for a in arrays]
    both = jnp.concatenate(arrays, axis=along)
    out = lax.psum_scatter(both, axis, scatter_dimension=dim, tiled=True)
    return tuple(jnp.split(out, [sum(widths[:k]) for k in range(1, len(widths))], axis=along))


def sent_together_2(arrays, axis, dim, along):
    widths = [math.prod(a.shape[along:]) for a in arrays]
    both = jnp.concatenate(
        [a.reshape(*a.shape[:along], w) for a, w in zip(arrays, widths)], axis=along
    )
    out = lax.psum_scatter(both, axis, scatter_dimension=dim, tiled=True)
    pieces = jnp.split(out, [sum(widths[:k]) for k in range(1, len(widths))], axis=along)
    return tuple((b.reshape(*out.shape[:along], *a.shape[along:]) for a, b in zip(arrays, pieces)))


def rms_norm(values, scaling):
    inv_rms = lax.rsqrt(jnp.mean(values * values, axis=-1, keepdims=True) + epsilon)
    return values * inv_rms * scaling


def rotary(values, places):
    half_size = values.shape[-1] // 2
    frequency = rope_base ** (-(2.0 / values.shape[-1]) * jnp.arange(half_size, dtype=jnp.float32))
    angles = places.astype(jnp.float32)[:, None] * frequency[None, :]
    cosines = jnp.cos(angles)[:, None, :]
    sines = jnp.sin(angles)[:, None, :]
    first_half = values[..., :half_size]
    second_half = values[..., half_size:]
    return jnp.concatenate(
        [first_half * cosines - second_half * sines, second_half * cosines + first_half * sines],
        axis=-1,
    )


def head_prepare(raw_heads, scaling, places):
    return rotary(rms_norm(raw_heads, scaling), places)


def slot_layout(route_rows, experts_all, capacity):
    flat_routes = route_rows.reshape(-1)
    onehot = (flat_routes[:, None] == jnp.arange(experts_all, dtype=jnp.int32)[None, :]).astype(
        jnp.int32
    )
    slot_rank = jnp.sum((jnp.cumsum(onehot, axis=0) - 1) * onehot, axis=1)
    slot_place = flat_routes * capacity + slot_rank
    source_row = (
        jnp.zeros((experts_all * capacity,), jnp.int32)
        .at[slot_place]
        .set(jnp.arange(flat_routes.shape[0], dtype=jnp.int32))
    )
    return (slot_place, source_row)


def expert_forward(received, gate_local, up_local, down_local):
    rows_flat = received.reshape(-1, received.shape[-1])
    gate_pre = jnp.dot(rows_flat, gate_local, preferred_element_type=jnp.float32)
    up_pre = jnp.dot(rows_flat, up_local, preferred_element_type=jnp.float32)
    hidden = (jax.nn.silu(gate_pre) * up_pre).astype(jnp.bfloat16)
    produced = jnp.dot(hidden, down_local, preferred_element_type=jnp.float32).astype(jnp.bfloat16)
    inner_shape = (received.shape[0], received.shape[1], gate_pre.shape[-1])
    return (
        produced.reshape(received.shape),
        received,
        gate_pre.reshape(inner_shape),
        up_pre.reshape(inner_shape),
    )


def attention_scores(grouped, key_all, visible_pairs, score_scale):
    scores = (
        jnp.einsum("qkgd,tkd->kgqt", grouped, key_all, preferred_element_type=jnp.float32)
        * score_scale
    )
    return jnp.where(visible_pairs[None, None], scores, masked_score)


def local(
    tokens,
    positions,
    routes,
    attn_gain,
    w_query,
    w_key,
    w_value,
    query_gain,
    key_gain,
    w_out,
    ffn_gain,
    w_router,
    w_gate,
    w_up,
    w_down,
    cotangent,
):
    ctx_count = lax.axis_size("ctx")
    experts_all = ctx_count * lax.axis_size("expert")
    capacity = TOK_DEV * TOP // experts_all
    group_size = HEADS // KV
    score_scale = HD ** (-0.5)
    (
        query_full,
        key_full,
        value_full,
        out_full,
        router_full,
        attn_scaling,
        ffn_scaling,
        query_scaling,
        key_scaling,
    ) = (
        *in_one_piece((w_query, w_key, w_value), ("ctx", "expert"), 0, 1),
        lax.all_gather(w_out, ("ctx", "expert"), axis=0, tiled=True),
        *side_by_side((w_router, attn_gain, ffn_gain), ("ctx", "expert"), 0, 1),
        lax.all_gather(query_gain, ("ctx", "expert"), axis=0, tiled=True),
        lax.all_gather(key_gain, ("ctx", "expert"), axis=0, tiled=True),
    )
    sequence = tokens[0].astype(jnp.float32)
    places_all = positions[0]
    ctx_offset = lax.axis_index("ctx") * TOK_DEV
    query_order = ctx_offset + jnp.arange(TOK_DEV, dtype=jnp.int32)
    key_order = jnp.arange(places_all.shape[0], dtype=jnp.int32)
    query_places = lax.dynamic_slice_in_dim(places_all, ctx_offset, TOK_DEV)
    visible_pairs = (key_order[None, :] <= query_order[:, None]) & (
        query_order[:, None] - key_order[None, :] == query_places[:, None] - places_all[None, :]
    )
    normed_attn, attn_norm_back = jax.vjp(rms_norm, sequence, attn_scaling.astype(jnp.float32))
    attn_low = normed_attn.astype(jnp.bfloat16)
    query_raw = jnp.dot(attn_low, query_full, preferred_element_type=jnp.float32).reshape(
        TOK_DEV, HEADS, HD
    )
    key_raw = jnp.dot(attn_low, key_full, preferred_element_type=jnp.float32).reshape(
        TOK_DEV, KV, HD
    )
    value_low = (
        jnp.dot(attn_low, value_full, preferred_element_type=jnp.float32)
        .astype(jnp.bfloat16)
        .reshape(TOK_DEV, KV, HD)
    )
    prepare_here = partial(head_prepare, places=query_places)
    query_rot, query_back = jax.vjp(prepare_here, query_raw, query_scaling.astype(jnp.float32))
    key_rot, key_back = jax.vjp(prepare_here, key_raw, key_scaling.astype(jnp.float32))
    grouped = query_rot.astype(jnp.bfloat16).reshape(TOK_DEV, KV, group_size, HD)
    key_local = key_rot.astype(jnp.bfloat16)
    key_all, value_all = in_one_piece((key_local, value_low), "ctx", 0, 1)
    scores = attention_scores(grouped, key_all, visible_pairs, score_scale)
    top_score = jnp.max(scores, axis=-1, keepdims=True)
    log_total = top_score + jnp.log(jnp.sum(jnp.exp(scores - top_score), axis=-1, keepdims=True))
    probs_low = jnp.exp(scores - log_total).astype(jnp.bfloat16)
    mixed = jnp.einsum("kgqt,tkd->qkgd", probs_low, value_all, preferred_element_type=jnp.float32)
    mixed = mixed.reshape(TOK_DEV, HEADS * HD).astype(jnp.bfloat16)
    after_attn = sequence + jnp.dot(mixed, out_full, preferred_element_type=jnp.float32)
    normed_ffn, ffn_norm_back = jax.vjp(rms_norm, after_attn, ffn_scaling.astype(jnp.float32))
    ffn_low = normed_ffn.astype(jnp.bfloat16)
    logits = jnp.dot(ffn_low, router_full, preferred_element_type=jnp.float32)
    route_rows = routes[0]
    route_onehot = (
        route_rows[:, :, None] == jnp.arange(experts_all, dtype=jnp.int32)[None, None, :]
    ).astype(jnp.float32)
    chosen = jnp.sum(route_onehot * logits[:, None, :], axis=2)
    gate_weights = jax.nn.softmax(chosen, axis=-1)
    slot_place, source_row = slot_layout(route_rows, experts_all, capacity)
    send_rows = ffn_low[source_row // TOP].reshape(experts_all, capacity, D)
    gate_local = w_gate[0]
    up_local = w_up[0]
    down_local = w_down[0]

    def expert_step(received):
        return expert_forward(received, gate_local, up_local, down_local)

    expert_out, received, gate_kept, up_kept = grouped_exchange(
        send_rows, ("ctx", "expert"), 0, 0, expert_step, 1, 1
    )
    returned = lax.all_to_all(
        expert_out, ("ctx", "expert"), split_axis=0, concat_axis=0, tiled=True
    )
    route_out = returned.reshape(-1, D)[slot_place].reshape(TOK_DEV, TOP, D).astype(jnp.float32)
    block_out = after_attn + jnp.sum(gate_weights[:, :, None] * route_out, axis=1)
    upstream = cotangent[0].astype(jnp.float32)
    d_produced = (gate_weights[:, :, None] * upstream[:, None, :]).astype(jnp.bfloat16)
    d_gates = jnp.sum(route_out * upstream[:, None, :], axis=2)
    d_chosen = gate_weights * (d_gates - jnp.sum(gate_weights * d_gates, axis=1, keepdims=True))
    d_logits = jnp.sum(d_chosen[:, :, None] * route_onehot, axis=1)
    d_send = d_produced.reshape(-1, D)[source_row].reshape(experts_all, capacity, D)
    d_received = lax.all_to_all(
        d_send, ("ctx", "expert"), split_axis=0, concat_axis=0, tiled=True
    ).reshape(-1, D)
    rows_flat = received.reshape(-1, D)
    gate_pre = gate_kept.reshape(-1, FF)
    up_pre = up_kept.reshape(-1, FF)
    sigmoid_gate = jax.nn.sigmoid(gate_pre)
    activated = gate_pre * sigmoid_gate
    hidden = (activated * up_pre).astype(jnp.bfloat16)
    d_hidden = jnp.einsum("md,fd->mf", d_received, down_local, preferred_element_type=jnp.float32)
    grad_down = jnp.einsum("mf,md->fd", hidden, d_received, preferred_element_type=jnp.float32)
    d_gate_pre = (
        d_hidden * up_pre * sigmoid_gate * (1.0 + gate_pre * (1.0 - sigmoid_gate))
    ).astype(jnp.bfloat16)
    d_up_pre = (d_hidden * activated).astype(jnp.bfloat16)
    grad_gate = jnp.einsum("md,mf->df", rows_flat, d_gate_pre, preferred_element_type=jnp.float32)
    grad_up = jnp.einsum("md,mf->df", rows_flat, d_up_pre, preferred_element_type=jnp.float32)
    d_rows = (
        jnp.einsum("mf,df->md", d_gate_pre, gate_local, preferred_element_type=jnp.float32)
        + jnp.einsum("mf,df->md", d_up_pre, up_local, preferred_element_type=jnp.float32)
    ).astype(jnp.bfloat16)
    d_back = lax.all_to_all(
        d_rows.reshape(experts_all, capacity, D),
        ("ctx", "expert"),
        split_axis=0,
        concat_axis=0,
        tiled=True,
    )
    d_route_in = d_back.reshape(-1, D)[slot_place].reshape(TOK_DEV, TOP, D).astype(jnp.float32)
    router_float = router_full.astype(jnp.float32)
    d_normed_ffn = jnp.sum(d_route_in, axis=1) + jnp.einsum(
        "re,de->rd", d_logits, router_float, precision=highest
    )
    grad_router = jnp.einsum("rd,re->de", ffn_low.astype(jnp.float32), d_logits, precision=highest)
    d_after, grad_ffn_gain = ffn_norm_back(d_normed_ffn)
    d_after = d_after + upstream
    d_attn_low = d_after.astype(jnp.bfloat16)
    grad_out = jnp.einsum("rc,rd->cd", mixed, d_attn_low, preferred_element_type=jnp.float32)
    d_mixed = jnp.einsum(
        "rd,cd->rc", d_attn_low, out_full, preferred_element_type=jnp.float32
    ).astype(jnp.bfloat16)
    d_grouped = d_mixed.reshape(TOK_DEV, KV, group_size, HD)
    scores_again = attention_scores(grouped, key_all, visible_pairs, score_scale)
    probs = jnp.exp(scores_again - log_total)
    probs_again = probs.astype(jnp.bfloat16)
    d_probs = jnp.einsum("qkgd,tkd->kgqt", d_grouped, value_all, preferred_element_type=jnp.float32)
    value_part = jnp.einsum(
        "kgqt,qkgd->tkd", probs_again, d_grouped, preferred_element_type=jnp.float32
    )
    d_scores = (probs * (d_probs - jnp.sum(probs * d_probs, axis=-1, keepdims=True))).astype(
        jnp.bfloat16
    )
    d_queries = (
        jnp.einsum("kgqt,tkd->qkgd", d_scores, key_all, preferred_element_type=jnp.float32)
        * score_scale
    )
    key_part = (
        jnp.einsum("kgqt,qkgd->tkd", d_scores, grouped, preferred_element_type=jnp.float32)
        * score_scale
    )
    d_key_local, d_value_local = sent_together(
        (key_part.astype(jnp.bfloat16), value_part.astype(jnp.bfloat16)), "ctx", 0, 1
    )
    d_query_raw, grad_query_gain = query_back(d_queries.reshape(TOK_DEV, HEADS, HD))
    d_key_raw, grad_key_gain = key_back(d_key_local)
    query_grad_low = d_query_raw.reshape(TOK_DEV, HEADS * HD).astype(jnp.bfloat16)
    key_grad_low = d_key_raw.reshape(TOK_DEV, KV * HD).astype(jnp.bfloat16)
    value_grad_low = d_value_local.reshape(TOK_DEV, KV * HD).astype(jnp.bfloat16)
    grad_query = jnp.einsum(
        "rd,rc->dc", attn_low, query_grad_low, preferred_element_type=jnp.float32
    )
    grad_key = jnp.einsum("rd,rc->dc", attn_low, key_grad_low, preferred_element_type=jnp.float32)
    grad_value = jnp.einsum(
        "rd,rc->dc", attn_low, value_grad_low, preferred_element_type=jnp.float32
    )
    d_normed_attn = (
        jnp.einsum("rc,dc->rd", query_grad_low, query_full, preferred_element_type=jnp.float32)
        + jnp.einsum("rc,dc->rd", key_grad_low, key_full, preferred_element_type=jnp.float32)
        + jnp.einsum("rc,dc->rd", value_grad_low, value_full, preferred_element_type=jnp.float32)
    )
    d_sequence, grad_attn_gain = attn_norm_back(d_normed_attn)
    d_tokens = d_after + d_sequence
    (
        half_query,
        half_key,
        half_value,
        half_out,
        half_router,
        half_attn_gain,
        half_ffn_gain,
        half_query_gain,
        half_key_gain,
    ) = (
        *tuple(
            (
                part.astype(jnp.float32)
                for part in side_by_side_2(
                    (
                        grad_query.astype(jnp.bfloat16),
                        grad_key.astype(jnp.bfloat16),
                        grad_value.astype(jnp.bfloat16),
                    ),
                    "ctx",
                    0,
                    1,
                )
            )
        ),
        lax.psum_scatter(
            grad_out.astype(jnp.bfloat16), "ctx", scatter_dimension=0, tiled=True
        ).astype(jnp.float32),
        *tuple(
            (
                part.astype(jnp.float32)
                for part in sent_together_2(
                    (
                        grad_router.astype(jnp.bfloat16),
                        grad_attn_gain.astype(jnp.bfloat16),
                        grad_ffn_gain.astype(jnp.bfloat16),
                    ),
                    "ctx",
                    0,
                    1,
                )
            )
        ),
        lax.psum_scatter(
            grad_query_gain.astype(jnp.bfloat16), "ctx", scatter_dimension=0, tiled=True
        ).astype(jnp.float32),
        lax.psum_scatter(
            grad_key_gain.astype(jnp.bfloat16), "ctx", scatter_dimension=0, tiled=True
        ).astype(jnp.float32),
    )
    (
        shard_query,
        shard_key,
        shard_value,
        shard_out,
        shard_router,
        shard_attn_gain,
        shard_ffn_gain,
        shard_query_gain,
        shard_key_gain,
    ) = (
        *side_by_side_2((half_query, half_key, half_value), "expert", 0, 1),
        lax.psum_scatter(half_out, "expert", scatter_dimension=0, tiled=True),
        *sent_together_2((half_router, half_attn_gain, half_ffn_gain), "expert", 0, 1),
        lax.psum_scatter(half_query_gain, "expert", scatter_dimension=0, tiled=True),
        lax.psum_scatter(half_key_gain, "expert", scatter_dimension=0, tiled=True),
    )
    return (
        block_out[None],
        d_tokens[None],
        shard_attn_gain,
        shard_query,
        shard_key,
        shard_value,
        shard_query_gain,
        shard_key_gain,
        shard_out,
        shard_ffn_gain,
        shard_router,
        grad_gate[None],
        grad_up[None],
        grad_down[None],
    )


def solution(mesh):
    placed = (
        P("expert", "ctx", None),
        P("expert", None),
        P("expert", "ctx", None),
        P(("ctx", "expert")),
        P(("ctx", "expert"), None),
        P(("ctx", "expert"), None),
        P(("ctx", "expert"), None),
        P(("ctx", "expert")),
        P(("ctx", "expert")),
        P(("ctx", "expert"), None),
        P(("ctx", "expert")),
        P(("ctx", "expert"), None),
        P(("ctx", "expert"), None, None),
        P(("ctx", "expert"), None, None),
        P(("ctx", "expert"), None, None),
        P("expert", "ctx", None),
    )
    return jax.shard_map(
        local,
        mesh=mesh,
        in_specs=placed,
        out_specs=(
            P("expert", "ctx", None),
            P("expert", "ctx", None),
            P(("ctx", "expert")),
            P(("ctx", "expert"), None),
            P(("ctx", "expert"), None),
            P(("ctx", "expert"), None),
            P(("ctx", "expert")),
            P(("ctx", "expert")),
            P(("ctx", "expert"), None),
            P(("ctx", "expert")),
            P(("ctx", "expert"), None),
            P(("ctx", "expert"), None, None),
            P(("ctx", "expert"), None, None),
            P(("ctx", "expert"), None, None),
        ),
        check_vma=False,
    )
```

profile of v0, /device:TPU:0, one launch (start us, length us, event | category | flops | bytes accessed | tf_op | source)
XLA Modules:
  0.0 2077.4 jit_solution(5973911350195512813)
XLA Ops:
  12.3 69.0 %all-reduce.12 = (bf16[128]{0:T(256)(128)(2,1)S(1)}, bf16[128]{0:T(256)(128)(2,1)S(1)}) all-reduce(bf16[128]{0:T(256)(128)(2,1)S(1)} %dynamic-update-slice, bf16[128]{0:T(256)(128)(2,1)S(1)} %dynamic-update-slice.1), channel_id=1, replica_groups=mesh['ctx'=2,'expert'=64] {'ctx','expert'}, use_global_device_ids=true, to_apply=%add.4 | all-reduce | flops 256 | bytes 1024
  88.4 4.3 scatter_custom_fusion
  94.1 318.8 %all_gather.18 = bf16[2048,130]{1,0:T(8,128)(2,1)S(1)} all-gather(bf16[16,130]{1,0:T(8,128)(2,1)S(1)} %pad_maximum_fusion.10), channel_id=1, replica_groups=mesh['ctx'=2,'expert'=64] {'ctx','expert'}, dimensions={0}, use_global_device_ids=true | all-gather | bytes 536640 | tf_op jit(solution)/shard_map/all_gather | solution.py:34
  424.2 14.1 slice_bitcast_fusion
  438.3 22.6 %copy.125 = bf16[4096,2048]{1,0:T(8,128)(2,1)} copy(bf16[4096,2048]{0,1:T(8,128)(2,1)} %slice_bitcast_fusion) | data formatting | bytes 33554432 | tf_op jit(solution)/shard_map/dot_general | solution.py:206
  460.9 8.4 multiply_reduce_fusion.2
  487.8 8.6 multiply_reduce_fusion.5
  498.3 9.9 gather_fusion
  508.3 6.6 fusion.130
  514.9 33.0 %all_to_all.30 = bf16[128,4,2048]{2,1,0:T(4,128)(2,1)} all-to-all(bf16[128,4,2048]{2,1,0:T(4,128)(2,1)S(1)} %get-tuple-element.92), channel_id=1, replica_groups=mesh['ctx'=2,'expert'=64] {'ctx','expert'}, dimensions={0} | all-to-all | bytes 4194304 | tf_op jit(solution)/shard_map/all_to_all | solution.py:45
  547.9 7.3 all-to-all-start.1
  563.3 11.5 gather_fusion.2
  574.8 8.3 all-to-all-done.1
  583.1 7.7 all-to-all-start.3
  590.8 3.9 reshape.630
  594.8 4.5 fusion.32
  605.4 4.1 reshape.631
  609.5 3.9 reshape.628
  613.5 4.5 fusion.34
  624.1 4.1 reshape.629
  628.2 5.0 pad_maximum_fusion.1
  633.3 10.2 all-to-all-done.3
  643.5 8.1 all-to-all-start.2
  687.4 8.4 fusion.24
  699.3 5.0 fusion.5
  704.4 10.8 all-to-all-start.4
  718.2 11.6 gather_fusion.1
  729.8 4.9 fusion.3
  736.8 31.0 %all-to-all-done.4 = bf16[128,8,2048]{2,1,0:T(8,128)(2,1)} async-done(((bf16[128,8,2048]{2,1,0:T(8,128)(2,1)}), bf16[128,8,2048]{2,1,0:T(8,128)(2,1)}, u32[]{:S(2)}, u32[]{:S(2)}) %all-to-all-start.4) | async-done | bytes 4194336 | tf_op jit(solution)/shard_map/all_to_all | solution.py:283
  767.8 11.5 gather_fusion.3
  779.4 5.2 convert_reduce_fusion
  787.0 11.8 fusion.55
  808.3 4.2 all_to_all.31
  820.0 9.6 convolution_convert_fusion.1
  829.5 12.8 fusion
  849.6 19.6 pad_maximum_fusion
  870.7 9.5 convolution_convert_fusion
  882.7 18.6 reduce-scatter.22.cloned.1.call-done
  901.3 15.0 concatenate.67
  916.4 17.8 reduce-scatter.16.cloned.1.call-done
  934.2 11.4 convert_element_type.314
  948.1 9.3 convolution_bitcast_fusion
  957.4 8.9 convolution_bitcast_fusion.1
  966.4 12.4 fusion.13
  981.3 179.1 %all-reduce.11 = (f32[64]{0:T(128)S(1)}, f32[64]{0:T(128)S(1)}) all-reduce(f32[64]{0:T(128)S(1)} %get-tuple-element.125, f32[64]{0:T(128)S(1)} %get-tuple-element.124), channel_id=7, replica_groups=mesh['ctx'=2,'expert'=64] {'expert'}, use_global_device_ids=true, to_apply=%region_32.33.clone | all-reduce | flops 128 | bytes 1024
  1165.9 124.2 %reduce-scatter.20.cloned.1.call-done = f32[16,130]{1,0:T(8,128)} async-done(((f32[1024,130]{1,0:T(8,128)}), f32[16,130]{1,0:T(8,128)}) %reduce-scatter.20.cloned.1.call-update) | async-done | bytes 8336
  1293.4 390.7 %reduce-scatter.14.cloned.1.call-done = f32[16,5120]{1,0:T(8,128)} async-done(((f32[1024,5120]{1,0:T(8,128)}), f32[16,5120]{1,0:T(8,128)}) %reduce-scatter.14.cloned.1.call-update) | async-done | bytes 327696 | tf_op jit(solution)/shard_map/reduce_scatter | solution.py:80
  1687.2 382.9 %reduce-scatter.18.cloned.1.call-done = f32[32,2048]{1,0:T(8,128)} async-done(((f32[2048,2048]{1,0:T(8,128)}), f32[32,2048]{1,0:T(8,128)}) %reduce-scatter.18.cloned.1.call-update) | async-done | bytes 262160 | tf_op jit(solution)/shard_map/reduce_scatter | solution.py:407
  (315 shorter events, 154.6 us)
Async XLA Ops:
  7.2 595.1 %copy-start = (bf16[1,768,2048]{2,1,0:T(8,128)(2,1)S(1)}, bf16[1,768,2048]{2,1,0:T(8,128)(2,1)}, u32[]{:S(2)}) copy-start(bf16[1,768,2048]{2,1,0:T(8,128)(2,1)} %param.30) | copy-start | bytes 9437188
  7.2 85.5 %copy-start.70 = (s32[1,256]{1,0:T(1,128)S(1)}, s32[1,256]{1,0:T(1,128)}, u32[]{:S(2)}) copy-start(s32[1,256]{1,0:T(1,128)} %param.17) | copy-start | bytes 3076
  7.2 85.5 %copy-start.69 = (bf16[16,128]{1,0:T(8,128)(2,1)S(1)}, bf16[16,128]{1,0:T(8,128)(2,1)}, u32[]{:S(2)}) copy-start(bf16[16,128]{1,0:T(8,128)(2,1)} %param.27) | copy-start | bytes 12292
  7.2 407.7 %all-gather.3.cloned.1.call-start = ((), (), s32[]{:S(2)}) async-start(), calls=%async_computation.12 | async-start | bytes 21135360 | tf_op jit(solution)/shard_map/all_gather | solution.py:27
  9.1 478.7 %all-gather.5.cloned.1.call-start = ((), (), s32[]{:S(2)}) async-start(), calls=%async_computation.13 | async-start | bytes 16908288 | tf_op jit(solution)/shard_map/all_gather | solution.py:190
  81.3 397.2 %copy-start.65 = (f32[128]{0:T(128)}, f32[128]{0:T(128)S(1)}, u32[]{:S(2)}) copy-start(f32[128]{0:T(128)S(1)} %convert_element_type.260) | copy-start | bytes 1540
  81.3 388.0 %copy-start.67 = (f32[128]{0:T(128)}, f32[128]{0:T(128)S(1)}, u32[]{:S(2)}) copy-start(f32[128]{0:T(128)S(1)} %convert_element_type.264) | copy-start | bytes 1540
  88.3 326.2 %copy-start.61 = (s32[1024,1]{0,1:T(1,128)}, s32[1024,1]{0,1:T(1,128)S(1)}, u32[]{:S(2)}) copy-start(s32[1024,1]{0,1:T(1,128)S(1)} %compare_select_fusion) | copy-start | bytes 12292
  94.0 320.6 %copy-start.71 = (f32[128]{0:T(128)}, f32[128]{0:T(128)S(1)}, u32[]{:S(2)}) copy-start(f32[128]{0:T(128)S(1)} %fusion.72) | copy-start | bytes 1540
  414.4 61.4 %copy-start.48 = (f32[2048]{0:T(1024)}, f32[2048]{0:T(1024)S(1)}, u32[]{:S(2)}) copy-start(f32[2048]{0:T(1024)S(1)} %get-tuple-element.79) | copy-start | bytes 24580
  414.4 61.3 %copy-start.59 = (f32[128]{0:T(128)}, f32[128]{0:T(128)S(1)}, u32[]{:S(2)}) copy-start(f32[128]{0:T(128)S(1)} %fusion.115) | copy-start | bytes 1540
  414.6 69.2 %copy-start.42 = (pred[128,256]{0,1:T(8,128)(4,1)}, pred[128,256]{0,1:T(8,128)(4,1)S(1)}, u32[]{:S(2)}) copy-start(pred[128,256]{0,1:T(8,128)(4,1)S(1)} %fusion.104) | copy-start | bytes 98308
  414.8 63.8 %copy-start.44 = (f32[128,64]{0,1:T(8,128)}, f32[128,64]{0,1:T(8,128)S(1)}, u32[]{:S(2)}) copy-start(f32[128,64]{0,1:T(8,128)S(1)} %get-tuple-element.110) | copy-start | bytes 98308
  414.8 63.8 %copy-start.46 = (f32[128,64]{0,1:T(8,128)}, f32[128,64]{0,1:T(8,128)S(1)}, u32[]{:S(2)}) copy-start(f32[128,64]{0,1:T(8,128)S(1)} %get-tuple-element.111) | copy-start | bytes 98308
  475.8 5.8 copy-start.15
  475.8 5.8 copy-start.17
  547.9 7.3 copy-start.56
  547.9 35.2 %all-to-all-start.1 = ((bf16[128,4,2048]{2,1,0:T(4,128)(2,1)}), bf16[128,4,2048]{2,1,0:T(4,128)(2,1)}, u32[]{:S(2)}, u32[]{:S(2)}) async-start(bf16[128,4,2048]{2,1,0:T(4,128)(2,1)} %get-tuple-element.93), calls=%async_computation.1 | async-start | bytes 4194304 | tf_op jit(solution)/shard_map/all_to_all | solution.py:45
  583.1 60.4 %all-to-all-start.3 = ((bf16[128,8,2048]{2,1,0:T(8,128)(2,1)}), bf16[128,8,2048]{2,1,0:T(8,128)(2,1)}, u32[]{:S(2)}, u32[]{:S(2)}) async-start(bf16[128,8,2048]{2,1,0:T(8,128)(2,1)} %bitcast.288), calls=%async_computation.3 | async-start | bytes 8388608 | tf_op jit(solution)/shard_map/all_to_all | solution.py:262
  594.8 4.5 copy-start.73
  643.5 60.9 %all-to-all-start.2 = ((bf16[128,8,2048]{2,1,0:T(8,128)(2,1)}), bf16[128,8,2048]{2,1,0:T(8,128)(2,1)}, u32[]{:S(2)}, u32[]{:S(2)}) async-start(bf16[128,8,2048]{2,1,0:T(8,128)(2,1)} %pad_maximum_fusion.1), calls=%async_computation.2 | async-start | bytes 8388608 | tf_op jit(solution)/shard_map/all_to_all | solution.py:251
  687.4 8.4 copy-start.75
  704.4 10.9 copy-start.62
  704.4 10.9 copy-start.9
  704.4 63.5 %all-to-all-start.4 = ((bf16[128,8,2048]{2,1,0:T(8,128)(2,1)}), bf16[128,8,2048]{2,1,0:T(8,128)(2,1)}, u32[]{:S(2)}, u32[]{:S(2)}) async-start(bf16[128,8,2048]{2,1,0:T(8,128)(2,1)} %fusion.5), calls=%async_computation.4 | async-start | bytes 8388608 | tf_op jit(solution)/shard_map/all_to_all | solution.py:283
  715.2 165.1 %reduce-scatter.12.cloned.1.call-start = ((), (), s32[]{:S(2)}) async-start(), calls=%async_computation.14 | async-start | bytes 835584 | tf_op jit(solution)/shard_map/reduce_scatter | solution.py:89
  718.2 11.6 copy-start.21
  729.8 5.6 copy-start.2
  779.4 5.2 copy-start.11
  779.4 5.2 copy-start.20
  787.0 11.8 copy-start.12
  787.0 12.1 copy-start.29
  787.0 12.1 copy-start.43
  787.0 12.1 copy-start.51
  807.5 5.0 copy-start.45
  807.5 5.0 copy-start.47
  849.5 51.8 %reduce-scatter.22.cloned.1.call-start = ((), (), s32[]{:S(2)}) async-start(), calls=%async_computation.19 | async-start | bytes 31457280
  869.2 65.0 %reduce-scatter.16.cloned.1.call-start = ((), (), s32[]{:S(2)}) async-start(), calls=%async_computation.16 | async-start | bytes 25165824 | tf_op jit(solution)/shard_map/reduce_scatter | solution.py:370
  880.3 409.8 %reduce-scatter.20.cloned.1.call-start = ((), (), s32[]{:S(2)}) async-start(), calls=%async_computation.18 | async-start | bytes 1064960
  882.6 801.5 %reduce-scatter.14.cloned.1.call-start = ((), (), s32[]{:S(2)}) async-start(), calls=%async_computation.15 | async-start | bytes 21299200 | tf_op jit(solution)/shard_map/reduce_scatter | solution.py:80
  916.4 1153.7 %reduce-scatter.18.cloned.1.call-start = ((), (), s32[]{:S(2)}) async-start(), calls=%async_computation.17 | async-start | bytes 17039360 | tf_op jit(solution)/shard_map/reduce_scatter | solution.py:407
  948.1 9.3 copy-start.80
  957.4 9.0 copy-start.24
  957.4 9.0 copy-start.25
  957.4 9.0 copy-start.26
  957.4 9.0 copy-start.27
  966.4 196.6 %copy-start.72 = (f32[128]{0:T(128)S(1)}, f32[128]{0:T(128)}, u32[]{:S(2)}) copy-start(f32[128]{0:T(128)} %copy-done.71) | copy-start | bytes 1540
  966.4 1103.7 %copy-start.1 = (bf16[1,768,2048]{2,1,0:T(8,128)(2,1)S(1)}, bf16[1,768,2048]{2,1,0:T(8,128)(2,1)}, u32[]{:S(2)}) copy-start(bf16[1,768,2048]{2,1,0:T(8,128)(2,1)} %param.30) | copy-start | bytes 9437188
  (46 other events, 95.9 us)
Sparse Core Ops, SparseCore 0:
  11.6 90.4 all-gather.2
  105.2 80.3 all-gather.4
  849.6 9.1 reduce-scatter.11
  869.4 31.9 reduce-scatter.21
  903.6 30.5 reduce-scatter.15
  936.5 353.5 reduce-scatter.19
  1292.5 391.5 reduce-scatter.13
  1687.1 382.9 reduce-scatter.17
where the time goes:
time: 2090 us; the launch traced here: 2080 us
  waiting for transfers between devices  985 us (47%)
  blocking collectives  609 us (29%)
  local copies, waits for them, and re-layouts  180 us (9%)
  matrix products  154 us (7%)
  other arithmetic  98.2 us (5%)
  starting transfers between devices  34.2 us (2%)
    reduce_scatter x1, waiting for transfers between devices, side_by_side_2(): out = lax.psum_scatter(both, axis, scatter_dimension=dim, tiled=True)  391 us
    reduce_scatter x1, waiting for transfers between devices, local(): lax.psum_scatter(half_out, 'expert', scatter_dimension=0, tiled=True)  383 us
    all_gather x1, blocking collectives, side_by_side(): out, at, done = (lax.all_gather(both, axis, axis=dim, tiled=True), 0, [])  319 us
    unnamed x3, blocking collectives  251 us
    unnamed x10, waiting for transfers between devices  144 us
  transfers between devices with their start and end apart: 12, of which 8 were waited for; matrix products, arithmetic and copies ran while one was open for 15% of the time, Pallas kernels for 0%

commit v1 on v0

v1 whole, which is shorter than its diff:
```python
from functools import partial

import jax
import jax.numpy as jnp
from jax import lax
from jax.experimental import pallas as pl
from jax.experimental.pallas import tpu as pltpu
from jax.sharding import Mesh
from jax.sharding import PartitionSpec as P

D = 2048
HEADS = 32
KV = 4
HD = 128
FF = 768
TOP = 8
TOK = 128
EXPERTS = 128
CAP = 8
WIDE = D + 128

epsilon = 1e-06
rope_base = 1000000.0
masked_score = -1e30
score_scale = HD ** (-0.5)
f32 = jnp.float32
bf16 = jnp.bfloat16
EXP = ("z", "x", "y")
ALL = ("ctx", "z", "x", "y")
SWAP = [(0, 1), (1, 0)]


def dot(a, b):
    return lax.dot_general(a, b, (((1,), (0,)), ((), ())), preferred_element_type=f32)


def dot_nt(a, b):
    return lax.dot_general(a, b, (((1,), (1,)), ((), ())), preferred_element_type=f32)


def dot_tn(a, b):
    return lax.dot_general(a, b, (((0,), (0,)), ((), ())), preferred_element_type=f32)


def call(body, grid, in_specs, out_specs, out_shape, scratch=(), flops=0, moved=0, vmem=40):
    return pl.pallas_call(
        body,
        grid=grid,
        in_specs=in_specs,
        out_specs=out_specs,
        out_shape=out_shape,
        scratch_shapes=list(scratch),
        compiler_params=pltpu.CompilerParams(vmem_limit_bytes=vmem * 2**20),
        cost_estimate=pl.CostEstimate(flops=flops, bytes_accessed=moved, transcendentals=0),
    )


def whole(shape):
    return pl.BlockSpec(shape, lambda *_: (0,) * len(shape))


def shape_of(dims, kind):
    return jax.ShapeDtypeStruct(dims, kind)


SIDE = 2 * 4 * TOK
COLS = 4 * HD + 2 * HD


def chunk_of(w_ref, count):
    return jnp.concatenate(
        [w_ref[:, 16 * k : 16 * k + 16, :].reshape(256, COLS) for k in range(count)], axis=0
    )


def project_body(x_ref, inv_ref, gain_ref, w_ref, raw_ref, normed_ref):
    x = x_ref[...].reshape(SIDE, 512).astype(f32)
    normed = (x * inv_ref[...] * gain_ref[...]).astype(bf16)
    normed_ref[...] = normed
    part = dot(normed, chunk_of(w_ref, 2)).reshape(2, 4 * TOK, COLS)

    @pl.when(pl.program_id(0) == 0)
    def _():
        raw_ref[...] = part

    @pl.when(pl.program_id(0) > 0)
    def _():
        raw_ref[...] += part


def project(x_all, inv, gain, gathered):
    return call(
        project_body,
        (4,),
        [
            pl.BlockSpec((2, 4 * TOK, 512), lambda i: (0, 0, i)),
            whole((SIDE, 1)),
            pl.BlockSpec((1, 512), lambda i: (0, i)),
            pl.BlockSpec((16, 32, COLS), lambda i: (0, i, 0)),
        ],
        [whole((2, 4 * TOK, COLS)), pl.BlockSpec((SIDE, 512), lambda i: (0, i))],
        [shape_of((2, 4 * TOK, COLS), f32), shape_of((SIDE, D), bf16)],
        flops=2 * SIDE * D * COLS,
        moved=14 * 2**20,
    )(x_all, inv, gain, gathered)


def prepared(raw, gain, cosines, sines):
    inv = lax.rsqrt(jnp.mean(raw * raw, axis=-1, keepdims=True) + epsilon)
    normed = raw * inv * gain
    return normed * cosines + pltpu.roll(normed, HD // 2, 1) * sines


def prepared_back(d_rot, raw, gain, cosines, sines):
    inv = lax.rsqrt(jnp.mean(raw * raw, axis=-1, keepdims=True) + epsilon)
    unit = raw * inv
    d_normed = d_rot * cosines + pltpu.roll(d_rot * sines, HD // 2, 1)
    d_gain = jnp.sum(d_normed * unit, axis=0, keepdims=True)
    d_unit = d_normed * gain
    d_raw = inv * (d_unit - unit * jnp.mean(unit * d_unit, axis=-1, keepdims=True))
    return d_raw, d_gain


def softmax_of(query, key, bias):
    scores = dot_nt(query, key) * score_scale + bias
    weight = jnp.exp(scores - jnp.max(scores, axis=-1, keepdims=True))
    return weight * (1.0 / jnp.sum(weight, axis=-1, keepdims=True))


def stacked(x, count=4):
    return jnp.concatenate([x[:, h * HD : (h + 1) * HD] for h in range(count)], axis=0)


def attend_body(raw_ref, bias_ref, cos_ref, sin_ref, qg, kg, q_out, k_out, v_out, mixed_out):
    def of(ref):
        return ref[...].reshape(2 * TOK, ref.shape[-1])

    cosines, sines = of(cos_ref), of(sin_ref)
    raw = of(raw_ref)
    key = prepared(raw[:, 512:640], kg[...], cosines, sines).astype(bf16)
    value = raw[:, 640:768].astype(bf16)
    k_out[...] = key.reshape(2, TOK, HD)
    v_out[...] = value.reshape(2, TOK, HD)
    cosines, sines = (jnp.concatenate([t] * 4, axis=0) for t in (cosines, sines))
    query = prepared(stacked(raw), qg[...], cosines, sines).astype(bf16)
    probs = softmax_of(query, key, jnp.concatenate([bias_ref[0]] * 4, axis=0))
    mixed = dot(probs.astype(bf16), value).astype(bf16)
    for h in range(4):
        at, rows = slice(h * HD, (h + 1) * HD), slice(h * 2 * TOK, (h + 1) * 2 * TOK)
        q_out[:, :, at] = query[rows].reshape(2, TOK, HD)
        mixed_out[:, :, at] = mixed[rows].reshape(2, TOK, HD)


def by_sequence(width):
    return pl.BlockSpec((2, TOK, width), lambda r: (0, r, 0))


def rows_of(width, kind=bf16):
    return shape_of((2, 4 * TOK, width), kind)


def attend(raw, bias, cosines, sines, qg, kg):
    one = pl.BlockSpec((1, 2 * TOK, 2 * TOK), lambda r: (r, 0, 0))
    return call(
        attend_body,
        (4,),
        [by_sequence(COLS), one, by_sequence(HD), by_sequence(HD)] + [whole((1, HD))] * 2,
        [by_sequence(512), by_sequence(HD), by_sequence(HD), by_sequence(512)],
        [rows_of(512), rows_of(HD), rows_of(HD), rows_of(512)],
        flops=4 * 16 * 256 * 256 * 128,
        moved=8 * 2**20,
    )(raw, bias, cosines, sines, qg, kg)


def attend_back_body(
    raw_ref, q_ref, k_ref, v_ref, dm_ref, bias_ref, cos_ref, sin_ref, qg, kg,
    d_out, gq_out, gk_out,
):
    def of(ref):
        return ref[...].reshape(2 * TOK, ref.shape[-1])

    @pl.when(pl.program_id(0) == 0)
    def _():
        gq_out[...] = jnp.zeros_like(gq_out)
        gk_out[...] = jnp.zeros_like(gk_out)

    cosines, sines = of(cos_ref), of(sin_ref)
    raw, key, value = of(raw_ref), of(k_ref), of(v_ref)
    query, d_mixed = stacked(of(q_ref)), stacked(of(dm_ref))
    probs = softmax_of(query, key, jnp.concatenate([bias_ref[0]] * 4, axis=0))
    d_probs = dot_nt(d_mixed, value)
    d_value = dot_tn(probs.astype(bf16), d_mixed)
    spread = probs * d_probs
    d_scores = (spread - probs * jnp.sum(spread, axis=-1, keepdims=True)).astype(bf16)
    d_query = dot(d_scores, key) * score_scale
    d_key = dot_tn(d_scores, query)
    cos_all, sin_all = (jnp.concatenate([t] * 4, axis=0) for t in (cosines, sines))
    d_raw, gain_sum = prepared_back(d_query, stacked(raw), qg[...], cos_all, sin_all)
    d_raw = d_raw.astype(bf16)
    for h in range(4):
        at, rows = slice(h * HD, (h + 1) * HD), slice(h * 2 * TOK, (h + 1) * 2 * TOK)
        d_out[:, :, at] = d_raw[rows].reshape(2, TOK, HD)
    d_raw, d_gain = prepared_back(d_key * score_scale, raw[:, 512:640], kg[...], cosines, sines)
    d_out[:, :, 512:640] = d_raw.astype(bf16).reshape(2, TOK, HD)
    d_out[:, :, 640:768] = d_value.astype(bf16).reshape(2, TOK, HD)
    gq_out[...] += gain_sum
    gk_out[...] += d_gain


def attend_back(raw, query, key, value, d_mixed, bias, cosines, sines, qg, kg):
    one = pl.BlockSpec((1, 2 * TOK, 2 * TOK), lambda r: (r, 0, 0))
    return call(
        attend_back_body,
        (4,),
        [by_sequence(COLS), by_sequence(512), by_sequence(HD), by_sequence(HD), by_sequence(512)]
        + [one, by_sequence(HD), by_sequence(HD)]
        + [whole((1, HD))] * 2,
        [by_sequence(COLS), whole((1, HD)), whole((1, HD))],
        [rows_of(COLS), shape_of((1, HD), f32), shape_of((1, HD), f32)],
        flops=10 * 16 * 256 * 256 * 128,
        moved=10 * 2**20,
    )(raw, query, key, value, d_mixed, bias, cosines, sines, qg, kg)


def out_body(m_ref, w_ref, o_ref):
    o_ref[...] = dot(m_ref[0], w_ref[...].reshape(512, 1024)).astype(o_ref.dtype)


def out_project(mixed, gathered, half, kind):
    return call(
        out_body,
        (2,),
        [
            pl.BlockSpec((1, 512, 512), lambda j: (half, 0, 0)),
            pl.BlockSpec((16, 32, 1024), lambda j: (0, 4 + j, 0)),
        ],
        pl.BlockSpec((512, 1024), lambda j: (0, j)),
        shape_of((512, D), kind),
        flops=2 * 512 * 512 * 2048,
        moved=6 * 2**20,
    )(mixed, gathered)


def out_back_body(d_ref, w_ref, o_ref):
    w = w_ref[...]
    low = w[:, :32].reshape(512, 1024)
    high = w[:, 32:].reshape(512, 1024)
    o_ref[...] = (dot_nt(d_ref[:, :1024], low) + dot_nt(d_ref[:, 1024:], high)).astype(bf16)


def out_back(d_side, gathered):
    return call(
        out_back_body,
        (2,),
        [
            pl.BlockSpec((256, D), lambda i: (i, 0)),
            pl.BlockSpec((16, 64, 1024), lambda i: (0, 2, 0)),
        ],
        pl.BlockSpec((256, 512), lambda i: (i, 0)),
        shape_of((512, 512), bf16),
        flops=2 * 512 * 512 * 2048,
        moved=5 * 2**20,
    )(d_side, gathered)


def out_grad_body(m_ref, a_ref, b_ref, o_ref):
    o_ref[...] = (dot_tn(m_ref[0], a_ref[...]) + dot_tn(m_ref[1], b_ref[...])).astype(bf16)


def out_grad(mixed, d_side, d_other):
    block = pl.BlockSpec((512, 1024), lambda j: (0, j))
    return call(
        out_grad_body,
        (2,),
        [whole((2, 512, 512)), block, block],
        block,
        shape_of((512, D), bf16),
        flops=2 * 1024 * 512 * 2048,
        moved=7 * 2**20,
    )(mixed, d_side, d_other)


def two_halves(value):
    high = value.astype(bf16)
    low = (value - high.astype(f32)).astype(bf16)
    lane = lax.broadcasted_iota(jnp.int32, (value.shape[0], 128), 1)
    return jnp.where(lane < 64, high.astype(f32), low.astype(f32)).astype(bf16)


def dispatch_body(
    x_ref, own_ref, left_ref, right_ref, gain_ref, router_ref, named_ref, place_ref,
    after_ref, low_ref, gate_ref, send_ref, turned,
):
    @pl.when(pl.program_id(0) == 0)
    def _():
        moved = left_ref[...].astype(f32) + right_ref[...].astype(f32)
        after = x_ref[...].astype(f32) + (own_ref[...] + moved)
        after_ref[...] = after
        inv = lax.rsqrt(jnp.mean(after * after, axis=-1, keepdims=True) + epsilon)
        low = (after * inv * gain_ref[...]).astype(bf16)
        low_ref[...] = low
        logits = dot(low, router_ref[...])
        named = named_ref[...]
        kept = jnp.where(named > 0.0, logits, masked_score)
        weight = jnp.exp(kept - jnp.max(kept, axis=-1, keepdims=True)) * named
        gates = weight * (1.0 / jnp.sum(weight, axis=-1, keepdims=True))
        gate_ref[...] = gates
        turned[...] = gates.T

    place = place_ref[...]
    send_ref[:, :D] = dot(place, low_ref[...]).astype(bf16)
    at = pl.multiple_of(pl.program_id(0) * 16, 16)
    gates = turned[pl.ds(at, 16), :]
    spread = jnp.broadcast_to(gates[:, None, :], (16, 8, 128)).reshape(128, 128)
    send_ref[:, D:] = two_halves(jnp.sum(spread * place.astype(f32), axis=-1, keepdims=True))


def dispatch(x, own, left, right, gain, router, named, place):
    row = whole((TOK, D))
    return call(
        dispatch_body,
        (8,),
        [row, row, row, row, whole((1, D)), whole((D, 128)), whole((128, 128))]
        + [pl.BlockSpec((128, 128), lambda i: (i, 0))],
        [row, row, whole((128, 128)), pl.BlockSpec((128, WIDE), lambda i: (i, 0))],
        [
            shape_of((TOK, D), f32),
            shape_of((TOK, D), bf16),
            shape_of((128, 128), f32),
            shape_of((1024, WIDE), bf16),
        ],
        scratch=[pltpu.VMEM((128, 128), f32)],
        flops=2 * 1024 * 128 * 2048,
        moved=9 * 2**20,
    )(x, own, left, right, gain, router, named, place)


def expert_body(
    x_ref, dh_ref, wg_ref, wu_ref, rows_ref, hid_ref, hidw_ref, dg_ref, du_ref
):
    x = x_ref[:, :D]
    side = x_ref[:, D:].astype(f32)
    gate_weight = side[:, 0:1] + side[:, 64:65]
    gate = dot(x, wg_ref[...])
    up = dot(x, wu_ref[...])
    sig = 1.0 / (1.0 + jnp.exp(-gate))
    act = gate * sig
    hidden = (act * up).astype(bf16)
    hid_ref[...] = hidden
    hidden = hidden.astype(f32)
    hidw_ref[...] = (hidden * gate_weight).astype(bf16)
    d_hidden = dh_ref[...]
    rows_ref[:, D:] = two_halves(jnp.sum(hidden * d_hidden, axis=-1, keepdims=True))
    d_hidden = d_hidden * gate_weight
    d_gate = (d_hidden * up * sig * (1.0 + gate * (1.0 - sig))).astype(bf16)
    d_up = (d_hidden * act).astype(bf16)
    dg_ref[...] = d_gate
    du_ref[...] = d_up
    rows_ref[:, :D] = (dot_nt(d_gate, wg_ref[...]) + dot_nt(d_up, wu_ref[...])).astype(bf16)


def expert(rows, d_hidden, w_gate, w_up):
    wide = pl.BlockSpec((256, WIDE), lambda i: (i, 0))
    inner = pl.BlockSpec((256, FF), lambda i: (i, 0))
    return call(
        expert_body,
        (4,),
        [wide, inner, whole((D, FF)), whole((D, FF))],
        [wide, inner, inner, inner, inner],
        [shape_of((1024, WIDE), bf16)] + [shape_of((1024, FF), bf16)] * 4,
        flops=8 * 1024 * 2048 * 768,
        moved=24 * 2**20,
        vmem=48,
    )(rows, d_hidden, w_gate, w_up)


def in_grad_body(x_ref, dg_ref, du_ref, gate_ref, up_ref):
    gate_ref[...] = dot_tn(x_ref[...], dg_ref[...])
    up_ref[...] = dot_tn(x_ref[...], du_ref[...])


def in_grads(rows, d_gate, d_up):
    out = pl.BlockSpec((256, FF), lambda i: (i, 0))
    return call(
        in_grad_body,
        (8,),
        [pl.BlockSpec((1024, 256), lambda i: (0, i)), whole((1024, FF)), whole((1024, FF))],
        [out, out],
        [shape_of((D, FF), f32)] * 2,
        flops=4 * 1024 * 2048 * 768,
        moved=20 * 2**20,
    )(rows, d_gate, d_up)


def down_grad_body(h_ref, g_ref, o_ref):
    o_ref[...] = dot_tn(h_ref[...], g_ref[...])


def down_grad(hidden, g_rows):
    return call(
        down_grad_body,
        (4,),
        [whole((1024, FF)), pl.BlockSpec((1024, 512), lambda i: (0, i))],
        pl.BlockSpec((FF, 512), lambda i: (0, i)),
        shape_of((FF, D), f32),
        flops=2 * 1024 * 2048 * 768,
        moved=12 * 2**20,
    )(hidden, g_rows)


def combine_body(
    back_ref, turn_ref, gates_ref, after_ref, low_ref, gain_ref, router_ref, g_ref,
    d_after_ref, d_low_ref, d_router_ref, d_gain_ref, total, d_gates,
):
    step = pl.program_id(0)

    @pl.when(step == 0)
    def _():
        total[...] = jnp.zeros_like(total)
        d_gates[...] = jnp.zeros_like(d_gates)

    turn = turn_ref[...]
    total[...] += dot(turn, back_ref[:, :D])
    side = back_ref[:, D:].astype(f32)
    slot = lax.broadcasted_iota(jnp.int32, (256, 128), 0) + step * 256
    named = (slot // CAP) == lax.broadcasted_iota(jnp.int32, (256, 128), 1)
    high = jnp.where(named, side[:, 0:1], 0.0).astype(bf16)
    low = jnp.where(named, side[:, 64:65], 0.0).astype(bf16)
    d_gates[...] += dot(turn, high) + dot(turn, low)

    @pl.when(step == 3)
    def _():
        gates, got = gates_ref[...], d_gates[...]
        d_logits = gates * (got - jnp.sum(gates * got, axis=-1, keepdims=True))
        d_high = d_logits.astype(bf16)
        d_rest = (d_logits - d_high.astype(f32)).astype(bf16)
        router = router_ref[...]
        d_normed = total[...] + (dot_nt(d_high, router) + dot_nt(d_rest, router))
        rows = low_ref[...]
        d_router_ref[...] = dot_tn(rows, d_high) + dot_tn(rows, d_rest)
        after = after_ref[...]
        inv = lax.rsqrt(jnp.mean(after * after, axis=-1, keepdims=True) + epsilon)
        unit = after * inv
        d_gain_ref[...] = jnp.sum(d_normed * unit, axis=0, keepdims=True)
        d_unit = d_normed * gain_ref[...]
        d_after = g_ref[...].astype(f32) + inv * (
            d_unit - unit * jnp.mean(unit * d_unit, axis=-1, keepdims=True)
        )
        d_after_ref[...] = d_after
        d_low_ref[...] = d_after.astype(bf16)


def combine(back, turn, gates, after, low, gain, router, g):
    row = whole((TOK, D))
    return call(
        combine_body,
        (4,),
        [
            pl.BlockSpec((256, WIDE), lambda i: (i, 0)),
            pl.BlockSpec((128, 256), lambda i: (0, i)),
            whole((128, 128)),
            row,
            row,
            whole((1, D)),
            whole((D, 128)),
            row,
        ],
        [row, row, whole((D, 128)), whole((1, D))],
        [
            shape_of((TOK, D), f32),
            shape_of((TOK, D), bf16),
            shape_of((D, 128), f32),
            shape_of((1, D), f32),
        ],
        scratch=[pltpu.VMEM((TOK, D), f32), pltpu.VMEM((128, 128), f32)],
        flops=2 * 1024 * 128 * 2048,
        moved=9 * 2**20,
    )(back, turn, gates, after, low, gain, router, g)


def project_back_body(d_ref, w_ref, x_ref, inv_ref, own_ref, send_ref, gain_ref):
    part = dot_nt(d_ref[...].reshape(SIDE, COLS), chunk_of(w_ref, 2))
    own_ref[...] = part[:512]
    send_ref[...] = part[512:].astype(bf16)
    unit = x_ref[...].reshape(SIDE, 512).astype(f32) * inv_ref[...]
    gain_ref[...] = jnp.sum(part * unit, axis=0, keepdims=True)


def project_back(d_raw, gathered, x_all, inv):
    out = pl.BlockSpec((512, 512), lambda i: (0, i))
    return call(
        project_back_body,
        (4,),
        [
            whole((2, 512, COLS)),
            pl.BlockSpec((16, 32, COLS), lambda i: (0, i, 0)),
            pl.BlockSpec((2, 512, 512), lambda i: (0, 0, i)),
            whole((SIDE, 1)),
        ],
        [out, out, pl.BlockSpec((1, 512), lambda i: (0, i))],
        [shape_of((512, D), f32), shape_of((512, D), bf16), shape_of((1, D), f32)],
        flops=2 * SIDE * D * COLS,
        moved=14 * 2**20,
    )(d_raw, gathered, x_all, inv)


def project_grad_body(n_ref, d_ref, side_ref, o_ref):
    o_ref[:, :COLS] = dot_tn(n_ref[...], d_ref[...].reshape(SIDE, COLS)).astype(bf16)
    o_ref[:, COLS:] = side_ref[...].astype(bf16)


def project_grad(normed, d_raw, side):
    return call(
        project_grad_body,
        (4,),
        [
            pl.BlockSpec((SIDE, 512), lambda i: (0, i)),
            whole((2, 512, COLS)),
            pl.BlockSpec((512, 256), lambda i: (i, 0)),
        ],
        pl.BlockSpec((512, 1024), lambda i: (i, 0)),
        shape_of((D, 1024), bf16),
        flops=2 * SIDE * D * COLS,
        moved=10 * 2**20,
    )(normed, d_raw, side)


def grad_sum_body(x_ref, q_ref, kv_ref, rest_ref):
    total = jnp.sum(x_ref[0].astype(f32), axis=0)
    q_ref[...] = total[:, :512]

    @pl.when(pl.program_id(0) % 2 == 0)
    def _():
        kv_ref[0] = total[:, 512:COLS]

    @pl.when(pl.program_id(0) % 2 == 1)
    def _():
        kv_ref[0] += total[:, 512:COLS]

    @pl.when(pl.program_id(0) == 0)
    def _():
        rest_ref[...] = total[:, COLS:]

    @pl.when(pl.program_id(0) > 0)
    def _():
        rest_ref[...] += total[:, COLS:]


def grad_sum(parts):
    return call(
        grad_sum_body,
        (8,),
        [pl.BlockSpec((1, 16, 16, 1024), lambda i: (i, 0, 0, 0))],
        [
            pl.BlockSpec((16, 512), lambda i: (0, i)),
            pl.BlockSpec((1, 16, 256), lambda i: (i // 2, 0, 0)),
            whole((16, 256)),
        ],
        [shape_of((16, 4096), f32), shape_of((4, 16, 256), f32), shape_of((16, 256), f32)],
        moved=5 * 2**20,
    )(parts)


def around(step):
    return [(i, (i + step) % 4) for i in range(4)]


def ring_gather(x):
    h = x.shape[0] // 2
    after = lax.ppermute(x, "z", around(-1))
    before = lax.ppermute(x, "z", around(1))
    far_a = lax.ppermute(after[:h], "z", around(-1))
    far_b = lax.ppermute(before[h:], "z", around(1))
    return jnp.concatenate([x, after, far_a, far_b, before], axis=0)


def ring_sum(own, got):
    piece = [
        own[r * TOK : (r + 1) * TOK].astype(f32) + got[r * TOK : (r + 1) * TOK].astype(f32)
        for r in range(4)
    ]
    h = TOK // 2
    far = piece[2].astype(bf16)
    a = lax.ppermute(far[:h], "z", around(1))
    b = lax.ppermute(far[h:], "z", around(-1))
    right = jnp.concatenate([piece[1][:h] + a.astype(f32), piece[1][h:]], axis=0).astype(bf16)
    left = jnp.concatenate([piece[3][:h], piece[3][h:] + b.astype(f32)], axis=0).astype(bf16)
    return piece[0], lax.ppermute(right, "z", around(1)), lax.ppermute(left, "z", around(-1))


def local(
    tokens,
    positions,
    routes,
    attn_gain,
    w_query,
    w_key,
    w_value,
    query_gain,
    key_gain,
    w_out,
    ffn_gain,
    w_router,
    w_gate,
    w_up,
    w_down,
    cotangent,
):
    c = lax.axis_index("ctx")

    def swapped(x):
        return lax.ppermute(x, "ctx", SWAP)

    gain_columns = jnp.concatenate(
        [
            attn_gain[:, None],
            ffn_gain[:, None],
            jnp.pad(query_gain[:, None], ((0, 15), (0, 0))),
            jnp.pad(key_gain[:, None], ((0, 15), (0, 0))),
            jnp.zeros((16, 124), bf16),
        ],
        axis=1,
    )
    queries_of = w_query.reshape(16, 8, 512).transpose(1, 0, 2)
    keys_of = jnp.repeat(w_key.reshape(16, 4, HD).transpose(1, 0, 2), 2, axis=0)
    values_of = jnp.repeat(w_value.reshape(16, 4, HD).transpose(1, 0, 2), 2, axis=0)
    everyone = jnp.broadcast_to(
        jnp.concatenate([w_router, gain_columns], axis=1)[None], (8, 16, 256)
    )
    column = lax.all_to_all(
        jnp.concatenate([queries_of, keys_of, values_of, everyone], axis=2),
        ("ctx", "z"),
        0,
        0,
        tiled=True,
    )
    pack = jnp.concatenate([column.reshape(128, 1024), w_out[:, :1024], w_out[:, 1024:]], axis=0)
    gathered = lax.all_gather(pack, ("x", "y"), axis=0, tiled=False)

    x_own, g_own = tokens[0], cotangent[0]
    places_own = lax.dynamic_slice_in_dim(positions[0], c * TOK, TOK).astype(bf16)
    x_side = ring_gather(jnp.concatenate([x_own, jnp.tile(places_own[:, None], (1, 128))], axis=1))
    x_both = jnp.stack([x_side, swapped(x_side)])
    x_all, places = x_both[:, :, :D], x_both[:, :, D].astype(f32)
    x_float = x_all.astype(f32)
    inv = lax.rsqrt(jnp.mean(x_float * x_float, axis=-1) + epsilon)
    frequency = rope_base ** (-(2.0 / HD) * jnp.arange(HD // 2, dtype=f32))
    angles = places[:, :, None] * frequency
    cosines = jnp.concatenate([jnp.cos(angles)] * 2, axis=-1)
    sines = jnp.concatenate([-jnp.sin(angles), jnp.sin(angles)], axis=-1)
    line = jnp.arange(TOK, dtype=f32)
    order = jnp.concatenate([line + c * TOK, line + (1 - c) * TOK])
    places = places.reshape(2, 4, TOK).transpose(1, 0, 2).reshape(4, 2 * TOK)
    visible = (order[None, None, :] <= order[None, :, None]) & (
        order[None, :, None] - order[None, None, :] == places[:, :, None] - places[:, None, :]
    )
    bias = jnp.where(visible, 0.0, masked_score).astype(f32)
    inv = inv.reshape(SIDE, 1)

    named = jnp.sum(
        (routes[0][:, :, None] == jnp.arange(EXPERTS, dtype=jnp.int32)).astype(f32), axis=1
    )
    before = jnp.arange(TOK)[:, None] > jnp.arange(TOK)[None, :]
    rank = dot(before.astype(bf16), named.astype(bf16))
    slot_rank = jnp.arange(CAP, dtype=f32)
    turn = (
        (named[:, :, None] > 0.0) & (rank[:, :, None] == slot_rank[None, None, :])
    ).reshape(TOK, EXPERTS * CAP)
    turn = turn.astype(bf16)
    place = turn.T

    g_send = dot(place, g_own).astype(bf16).reshape(EXPERTS, CAP, D)
    g_rows = lax.all_to_all(g_send, ALL, 0, 0, tiled=True).reshape(-1, D)
    gate_local, up_local, down_local = w_gate[0], w_up[0], w_down[0]

    gathered, g_rows = lax.optimization_barrier((gathered, g_rows))
    d_hidden_raw = dot_nt(g_rows, down_local)
    small = gathered[:, :128, COLS:].reshape(16, 8, 16, 256).transpose(1, 0, 2, 3).reshape(D, 256)
    router_full = small[:, :128]
    gains = small[:, 128:132].astype(f32)
    attn_scale = gains[:, 0].reshape(1, D)
    ffn_scale = gains[:, 1].reshape(1, D)
    qg = gains[:, 2].reshape(HD, 16)[:, 0].reshape(1, HD)
    kg = gains[:, 3].reshape(HD, 16)[:, 0].reshape(1, HD)

    raw, normed = project(x_all, inv, attn_scale, gathered)
    query, key, value, mixed = attend(raw, bias, cosines, sines, qg, kg)
    out_got = swapped(out_project(mixed, gathered, 1, bf16))
    out_own = out_project(mixed, gathered, 0, f32)
    out_pieces = ring_sum(out_own, out_got)

    after, ffn_low, gates, send = dispatch(
        x_own, *out_pieces, ffn_scale, router_full, named, place
    )
    received = lax.all_to_all(send.reshape(EXPERTS, CAP, WIDE), ALL, 0, 0, tiled=True)
    received = received.reshape(-1, WIDE)
    d_rows, hidden, hidden_w, d_gate, d_up = expert(received, d_hidden_raw, gate_local, up_local)
    back = lax.all_to_all(d_rows.reshape(EXPERTS, CAP, WIDE), ALL, 0, 0, tiled=True)
    back = back.reshape(-1, WIDE)
    produced = dot(hidden, down_local).astype(bf16)
    grad_gate, grad_up = in_grads(received, d_gate, d_up)
    grad_down = down_grad(hidden_w, g_rows)

    d_after, d_attn, d_router, d_ffn_gain = combine(
        back, turn, gates, after, ffn_low, ffn_scale, router_full, g_own
    )
    d_side = ring_gather(d_attn)
    produced, d_side = lax.optimization_barrier((produced, d_side))
    returned = lax.all_to_all(produced.reshape(EXPERTS, CAP, D), ALL, 0, 0, tiled=True)
    returned = returned.reshape(-1, D)
    weighted = jnp.repeat(gates, CAP, axis=1) * turn.astype(f32)
    weighted_high = weighted.astype(bf16)
    weighted_rest = (weighted - weighted_high.astype(f32)).astype(bf16)
    block_out = after + (dot(weighted_high, returned) + dot(weighted_rest, returned))

    d_other = swapped(d_side)
    d_mixed = jnp.stack([out_back(d_side, gathered), out_back(d_other, gathered)])
    grad_out = out_grad(mixed, d_side, d_other)
    grad_out = lax.all_to_all(grad_out.reshape(16, 32, D), ("x", "y"), 0, 0, tiled=True)
    grad_out = jnp.sum(grad_out.astype(f32), axis=0)

    d_raw, d_query_gain, d_key_gain = attend_back(
        raw, query, key, value, d_mixed, bias, cosines, sines, qg, kg
    )
    d_own, d_send, d_attn_gain = project_back(d_raw, gathered, x_all, inv)
    d_pieces = ring_sum(d_own, swapped(d_send))
    d_normed = d_pieces[0] + d_pieces[1].astype(f32) + d_pieces[2].astype(f32)
    inv_own = inv[:TOK]
    unit = x_own.astype(f32) * inv_own
    d_unit = d_normed * attn_scale
    d_tokens = d_after + inv_own * (
        d_unit - unit * jnp.mean(unit * d_unit, axis=-1, keepdims=True)
    )

    per_chip = jnp.zeros((128, 16, 2), f32)
    per_chip = per_chip.at[:, 0, 0].set(d_query_gain[0]).at[:, 0, 1].set(d_key_gain[0])
    side = jnp.concatenate(
        [
            d_router,
            d_attn_gain.reshape(D, 1),
            d_ffn_gain.reshape(D, 1),
            per_chip.reshape(D, 2),
            jnp.zeros((D, 124), f32),
        ],
        axis=1,
    )
    sums = project_grad(normed, d_raw, side).reshape(128, 16, 1024)
    sums = lax.all_to_all(sums, ALL, 0, 0, tiled=True).reshape(8, 16, 16, 1024)
    grad_query, pair, rest = grad_sum(sums)
    grad_key = pair[:, :, :HD].transpose(1, 0, 2).reshape(16, 512)
    grad_value = pair[:, :, HD:].transpose(1, 0, 2).reshape(16, 512)

    return (
        block_out[None],
        d_tokens[None],
        rest[:, 128],
        grad_query,
        grad_key,
        grad_value,
        rest[0, 130:131],
        rest[0, 131:132],
        grad_out,
        rest[:, 129],
        rest[:, :128],
        grad_gate[None],
        grad_up[None],
        grad_down[None],
    )


def solution(mesh):
    chips = Mesh(mesh.devices.reshape(2, 4, 4, 4), ALL)
    tokens = P(EXP, "ctx", None)
    row = P(ALL, None)
    line = P(ALL)
    stack = P(ALL, None, None)
    placed = (
        tokens, P(EXP, None), tokens, line, row, row, row, line, line, row, line, row,
        stack, stack, stack, tokens,
    )
    given = (
        tokens, tokens, line, row, row, row, line, line, row, line, row, stack, stack, stack,
    )
    return jax.shard_map(local, mesh=chips, in_specs=placed, out_specs=given, check_vma=False)
```

time: 2090 us -> 596 us (0.29)
  waiting for transfers between devices: 985 us -> 185 us
  blocking collectives: 609 us -> 100 us
  matrix products: 154 us -> 23.8 us
  local copies, waits for them, and re-layouts: 180 us -> 71.4 us
  Pallas kernels: 0 us -> 99.6 us
  other arithmetic: 98.2 us -> 26.9 us
  starting transfers between devices: 34.2 us -> 65.4 us
    reduce_scatter x4 -> x0, waiting for transfers between devices: 791 us -> none  [the longest x1 391 us: side_by_side_2(): out = lax.psum_scatter(both, axis, scatter_dimension=dim, tiled=True)]
    all_gather x2 -> x0, blocking collectives: 321 us -> none  [the longest x1 319 us: side_by_side(): out, at, done = (lax.all_gather(both, axis, axis=dim, tiled=True), 0, [])]
    unnamed x3 -> x0, blocking collectives: 251 us -> none
    unnamed x10 -> x1, waiting for transfers between devices: 144 us -> 0.02 us
    dot_general x33 -> x6, matrix products: 154 us -> 23.8 us  [the longest x5 16.5 us: dot(): lax.dot_general(a, b, (((1,), (0,)), ((), ())), preferred_element_type=f32)]
    ppermute x0 -> x20, waiting for transfers between devices: none -> 122 us  [the longest x2 45.2 us: ring_gather(): far_a = lax.ppermute(after[:h], 'z', around(-1))]
    pallas_call x0 -> x16, Pallas kernels: none -> 99.6 us  [the longest x1 18.9 us: expert(): call(expert_body, (4,), [wide, inner, whole((D, FF)), whole((D, FF))], [w...]
    all_to_all x2, blocking collectives: 37.2 us -> 100 us  [the longest x1 66.1 us: local(): lax.all_to_all(d_rows.reshape(EXPERTS, CAP, WIDE), ALL, 0, 0, tiled=True)]
  transfers between devices with their start and end apart: 12 -> 26, of which waited for: 8 -> 16; matrix products, arithmetic and copies ran while one was open for 15% -> 13% of each run, Pallas kernels for 0% -> 7%
where the time goes in v1:
time: 596 us; the launch traced here: 589 us
  waiting for transfers between devices  185 us (31%)
  blocking collectives  100 us (17%)
  Pallas kernels  99.6 us (17%)
  local copies, waits for them, and re-layouts  71.4 us (12%)
  starting transfers between devices  65.4 us (11%)
  other arithmetic  26.9 us (5%)
  matrix products  23.8 us (4%)
  between operations  16.7 us (3%)
    all_to_all x1, blocking collectives, local(): lax.all_to_all(d_rows.reshape(EXPERTS, CAP, WIDE), ALL, 0, 0, tiled=True)  66.1 us
    all_to_all x1, waiting for transfers between devices, local(): lax.all_to_all(send.reshape(EXPERTS, CAP, WIDE), ALL, 0, 0, tiled=True)  48.5 us
    ppermute x2, waiting for transfers between devices, ring_gather(): far_a = lax.ppermute(after[:h], 'z', around(-1))  45.2 us
    ppermute x2, waiting for transfers between devices, ring_sum(): b = lax.ppermute(far[h:], 'z', around(-1))  40.4 us
    unnamed x156, local copies, waits for them, and re-layouts  35.4 us
    all_to_all x1, blocking collectives, local(): lax.all_to_all(grad_out.reshape(16, 32, D), ('x', 'y'), 0, 0, tiled=True)  34.3 us
    pallas_call x1, Pallas kernels, expert(): call(expert_body, (4,), [wide, inner, whole((D, FF)), whole((D, FF))], [w...  18.9 us
    dot_general x5, matrix products, dot(): lax.dot_general(a, b, (((1,), (0,)), ((), ())), preferred_element_type=f32)  16.5 us
  transfers between devices with their start and end apart: 26, of which 16 were waited for; matrix products, arithmetic and copies ran while one was open for 13% of the time, Pallas kernels for 7%

profile of v1, /device:TPU:0, one launch (start us, length us, event | category | flops | bytes accessed | tf_op | source)
XLA Modules:
  0.0 588.7 jit_solution(5979027783037271888)
XLA Ops:
  14.4 5.4 all-to-all-start
  20.7 6.0 %all-to-all-done = bf16[8,16,1024]{2,1,0:T(8,128)(2,1)S(1)} async-done(((bf16[8,16,1024]{2,1,0:T(8,128)(2,1)}), bf16[8,16,1024]{2,1,0:T(8,128)(2,1)S(1)}, u32[]{:S(2)}, u32[]{:S(2)}) %all-to-all-start) | async-done | bytes 262176 | tf_op jit(solution)/shard_map/all_to_all | solution.py:630
  32.5 4.3 convert_bitcast_fusion
  36.8 10.6 %all-to-all-start.1 = ((bf16[128,8,2048]{2,1,0:T(8,128)(2,1)}), bf16[128,8,2048]{2,1,0:T(8,128)(2,1)}, u32[]{:S(2)}, u32[]{:S(2)}) async-start(bf16[128,8,2048]{2,1,0:T(8,128)(2,1)} %convert_bitcast_fusion), calls=%async_computation.1 | async-start | bytes 8388608 | tf_op jit(solution)/shard_map/all_to_all | solution.py:673
  48.4 2.8 collective-permute-start.1
  54.2 40.3 %collective-permute-done.1 = bf16[64,2176]{1,0:T(8,128)(2,1)S(1)} collective-permute-done((bf16[64,2176]{1,0:T(8,128)(2,1)S(1)}, bf16[64,2176]{1,0:T(8,128)(2,1)S(1)}, u32[]{:S(2)}, u32[]{:S(2)}) %collective-permute-start.1) | collective-permute-done | bytes 278560 | tf_op jit(solution)/shard_map/ppermute | solution.py:572
  99.2 3.7 collective-permute-done.4
  102.9 4.1 multiply_reduce_fusion
  113.7 8.0 %all-gather.3.cloned.1.call-done = bf16[3072,1024]{1,0:T(8,128)(2,1)} async-done(((bf16[192,1024]{1,0:T(8,128)(2,1)}), bf16[3072,1024]{1,0:T(8,128)(2,1)}) %all-gather.3.cloned.1.call-update) | async-done | bytes 6291472 | tf_op jit(solution)/shard_map/all_gather | solution.py:638
  129.8 7.6 %shard_map.263 = (f32[2,512,768]{2,1,0:T(8,128)S(1)}, bf16[1024,2048]{1,0:T(8,128)(2,1)S(1)}) custom-call(bf16[2,512,2048]{2,1,0:T(8,128)(2,1)S(1)} %copy-done.5, f32[1024,1]{1,0:T(8,128)S(1)} %copy-done.38, f32[1,2048]{1,0:T(1,128)S(1)} %bitcast.132, bf16[16,192,1024]{2,1,0:T(8,128)(2,1)} %bitcast.116), custom_call_target="tpu_custom_call" | custom-call | flops 3221225472 | bytes 14680064 | tf_op jit(solution)/shard_map/pallas_call | solution.py:92
  139.4 11.4 %shard_map.264 = (bf16[2,512,512]{2,1,0:T(8,128)(2,1)S(1)}, bf16[2,512,128]{2,1,0:T(8,128)(2,1)S(1)}, bf16[2,512,128]{2,1,0:T(8,128)(2,1)S(1)}, bf16[2,512,512]{2,1,0:T(8,128)(2,1)S(1)}) custom-call(f32[2,512,768]{2,1,0:T(8,128)S(1)} %get-tuple-element.73.raw_ref, f32[4,256,256]{2,1,0:T(8,128)S(1)} %copy-done.9, f32[2,512,128]{2,1,0:T(8,128)S(1)} %copy-done.20, ...), custom_call_target="tpu_custom_call" | custom-call | flops 536870912 | bytes 8388608 | tf_op jit(solution)/shard_map/pallas_call | solution.py:164
  151.8 3.3 copy-done.2
  163.0 3.2 collective-permute-start.6
  167.8 6.5 %collective-permute-done.6 = bf16[64,2048]{1,0:T(8,128)(2,1)S(1)} collective-permute-done((bf16[64,2048]{1,0:T(8,128)(2,1)S(1)}, bf16[64,2048]{1,0:T(8,128)(2,1)S(1)}, u32[]{:S(2)}, u32[]{:S(2)}) %collective-permute-start.6) | collective-permute-done | bytes 262176 | tf_op jit(solution)/shard_map/ppermute | solution.py:584
  176.5 3.0 collective-permute-start.9
  187.1 3.2 collective-permute-done.7.left_ref
  193.7 4.5 shard_map.267
  202.1 9.8 %all-to-all-start.2 = ((bf16[128,8,2176]{2,1,0:T(8,128)(2,1)}), bf16[128,8,2176]{2,1,0:T(8,128)(2,1)}, u32[]{:S(2)}, u32[]{:S(2)}) async-start(bf16[128,8,2176]{2,1,0:T(8,128)(2,1)} %bitcast.126), calls=%async_computation.2 | async-start | bytes 8912896 | tf_op jit(solution)/shard_map/all_to_all | solution.py:695
  211.9 7.3 %fusion.2.dh_ref = f32[1024,768]{1,0:T(8,128)} fusion(bf16[1024,2048]{1,0:T(8,128)(2,1)} %bitcast.19.g_ref, bf16[1,768,2048]{2,1,0:T(8,128)(2,1)S(1)} %copy-done), kind=kOutput, calls=%fused_computation.8 | convolution fusion | flops 3221225472 | bytes 10485760 | tf_op jit(solution)/shard_map/dot_general | solution.py:38
  219.2 48.5 %all-to-all-done.2 = bf16[128,8,2176]{2,1,0:T(8,128)(2,1)} async-done(((bf16[128,8,2176]{2,1,0:T(8,128)(2,1)}), bf16[128,8,2176]{2,1,0:T(8,128)(2,1)}, u32[]{:S(2)}, u32[]{:S(2)}) %all-to-all-start.2) | async-done | bytes 4456480 | tf_op jit(solution)/shard_map/all_to_all | solution.py:695
  267.8 18.9 %shard_map.268 = (bf16[1024,2176]{1,0:T(8,128)(2,1)}, bf16[1024,768]{1,0:T(8,128)(2,1)S(1)}, bf16[1024,768]{1,0:T(8,128)(2,1)S(1)}, bf16[1024,768]{1,0:T(8,128)(2,1)S(1)}, bf16[1024,768]{1,0:T(8,128)(2,1)}) custom-call(bf16[1024,2176]{1,0:T(8,128)(2,1)} %bitcast.30.x_ref, f32[1024,768]{1,0:T(8,128)} %fusion.2.dh_ref, bf16[2048,768]{1,0:T(8,128)(2,1)} %bitcast.167, ...), custom_call_target="tpu_custom_call" | custom-call | flops 12884901888 | bytes 25165824 | tf_op jit(solution)/shard_map/pallas_call | solution.py:365
  287.9 66.1 %all_to_all.35 = bf16[128,8,2176]{2,1,0:T(8,128)(2,1)S(1)} all-to-all(bf16[128,8,2176]{2,1,0:T(8,128)(2,1)} %bitcast.146), channel_id=1, replica_groups=mesh['ctx'=2,'z'=4,'x'=4,'y'=4] {'ctx','z','x','y'}, dimensions={0} | all-to-all | bytes 8912896 | tf_op jit(solution)/shard_map/all_to_all | solution.py:698
  354.0 2.8 shard_map.269
  359.1 4.9 convolution_convert_fusion
  364.0 6.5 %collective-permute-done.10 = bf16[128,2048]{1,0:T(8,128)(2,1)S(1)} collective-permute-done((bf16[128,2048]{1,0:T(8,128)(2,1)S(1)}, bf16[128,2048]{1,0:T(8,128)(2,1)S(1)}, u32[]{:S(2)}, u32[]{:S(2)}) %collective-permute-start.10) | collective-permute-done | bytes 524320 | tf_op jit(solution)/shard_map/ppermute | solution.py:570
  372.8 4.9 collective-permute-done.11
  377.7 2.6 collective-permute-done.13
  380.5 4.1 collective-permute-done.14.d_ref.b_ref
  384.7 3.0 shard_map.276
  387.7 34.3 %all_to_all.36 = bf16[16,32,2048]{2,1,0:T(8,128)(2,1)} all-to-all(bf16[16,32,2048]{2,1,0:T(8,128)(2,1)S(1)} %bitcast.129), channel_id=1, replica_groups=mesh['ctx'=2,'z'=4,'x'=4,'y'=4] {'x','y'}, dimensions={0} | all-to-all | bytes 4194304 | tf_op jit(solution)/shard_map/all_to_all | solution.py:719
  422.0 6.0 %all-to-all-start.4 = ((bf16[128,8,2048]{2,1,0:T(8,128)(2,1)}), bf16[128,8,2048]{2,1,0:T(8,128)(2,1)}, u32[]{:S(2)}, u32[]{:S(2)}) async-start(bf16[128,8,2048]{2,1,0:T(8,128)(2,1)} %bitcast.150), calls=%async_computation.4 | async-start | bytes 8388608 | tf_op jit(solution)/shard_map/all_to_all | solution.py:709
  428.0 2.8 copy-done.3
  435.8 8.1 %shard_map.272 = (bf16[2,512,768]{2,1,0:T(8,128)(2,1)S(1)}, f32[1,128]{1,0:T(1,128)S(1)}, f32[1,128]{1,0:T(1,128)S(1)}) custom-call(f32[2,512,768]{2,1,0:T(8,128)S(1)} %copy-done.8, bf16[2,512,512]{2,1,0:T(8,128)(2,1)S(1)} %copy-done.43, bf16[2,512,128]{2,1,0:T(8,128)(2,1)S(1)} %copy-done.52, bf16[2,512,128]{2,1,0:T(8,128)(2,1)S(1)} %copy-done.54, ...), custom_call_target="tpu_custom_call" | custom-call | flops 1342177280 | bytes 10485760 | tf_op jit(solution)/shard_map/pallas_call | solution.py:212
  444.0 7.3 %shard_map.273 = (f32[512,2048]{1,0:T(8,128)S(1)}, bf16[512,2048]{1,0:T(8,128)(2,1)}, f32[1,2048]{1,0:T(1,128)S(1)}) custom-call(bf16[2,512,768]{2,1,0:T(8,128)(2,1)S(1)} %get-tuple-element.89.d_ref, bf16[16,192,1024]{2,1,0:T(8,128)(2,1)} %bitcast.117, bf16[2,512,2048]{2,1,0:T(8,128)(2,1)S(1)} %copy-done.6, f32[1024,1]{1,0:T(8,128)S(1)} %copy-done.39), custom_call_target="tpu_custom_call" | custom-call | flops 3221225472 | bytes 14680064 | tf_op jit(solution)/shard_map/pallas_call | solution.py:491
  454.7 11.1 %shard_map.277 = (f32[2048,768]{1,0:T(8,128)}, f32[2048,768]{1,0:T(8,128)}) custom-call(bf16[1024,2176]{1,0:T(8,128)(2,1)} %bitcast.30.x_ref, bf16[1024,768]{1,0:T(8,128)(2,1)S(1)} %copy-done.60, bf16[1024,768]{1,0:T(8,128)(2,1)S(1)} %copy-done.61), custom_call_target="tpu_custom_call" | custom-call | flops 6442450944 | bytes 20971520 | tf_op jit(solution)/shard_map/pallas_call | solution.py:384
  472.6 3.4 concatenate.64.side_ref
  479.7 4.5 shard_map.274
  486.2 2.9 convert_add_fusion.1
  489.1 10.4 %all-to-all-start.5 = ((bf16[128,16,1024]{2,1,0:T(8,128)(2,1)}), bf16[128,16,1024]{2,1,0:T(8,128)(2,1)}, u32[]{:S(2)}, u32[]{:S(2)}) async-start(bf16[128,16,1024]{2,1,0:T(8,128)(2,1)} %bitcast.123), calls=%async_computation.5 | async-start | bytes 8388608 | tf_op jit(solution)/shard_map/all_to_all | solution.py:748
  499.5 2.8 collective-permute-start.18
  502.3 7.4 %shard_map.278 = f32[768,2048]{1,0:T(8,128)} custom-call(bf16[1024,768]{1,0:T(8,128)(2,1)S(1)} %copy-done.41, bf16[1024,2048]{1,0:T(8,128)(2,1)} %bitcast.19.g_ref), custom_call_target="tpu_custom_call" | custom-call | flops 3221225472 | bytes 12582912 | tf_op jit(solution)/shard_map/pallas_call | solution.py:400
  511.1 40.3 %collective-permute-done.18 = bf16[64,2048]{1,0:T(8,128)(2,1)S(1)} collective-permute-done((bf16[64,2048]{1,0:T(8,128)(2,1)S(1)}, bf16[64,2048]{1,0:T(8,128)(2,1)S(1)}, u32[]{:S(2)}, u32[]{:S(2)}) %collective-permute-start.18) | collective-permute-done | bytes 262176 | tf_op jit(solution)/shard_map/ppermute | solution.py:585
  553.9 3.0 convolution_bitcast_fusion
  556.9 4.1 fusion.6
  561.0 4.3 collective-permute-done.19
  565.2 3.1 collective-permute-done.17
  569.9 2.5 add_bitcast_fusion
  572.4 6.1 %shard_map.275 = (f32[16,4096]{1,0:T(8,128)}, f32[4,16,256]{2,1,0:T(8,128)S(1)}, f32[16,256]{1,0:T(8,128)S(1)}) custom-call(bf16[8,16,16,1024]{3,2,1,0:T(8,128)(2,1)} %bitcast.52.x_ref), custom_call_target="tpu_custom_call" | custom-call | bytes 5242880 | tf_op jit(solution)/shard_map/pallas_call | solution.py:550
  (280 shorter events, 100.3 us)
Async XLA Ops:
  7.2 204.8 %copy-start = (bf16[1,768,2048]{2,1,0:T(8,128)(2,1)S(1)}, bf16[1,768,2048]{2,1,0:T(8,128)(2,1)}, u32[]{:S(2)}) copy-start(bf16[1,768,2048]{2,1,0:T(8,128)(2,1)} %param.34) | copy-start | bytes 9437188
  7.2 20.3 %copy-start.72 = (s32[1,256]{1,0:T(1,128)S(1)}, s32[1,256]{1,0:T(1,128)}, u32[]{:S(2)}) copy-start(s32[1,256]{1,0:T(1,128)} %param.21) | copy-start | bytes 3076
  13.5 18.2 %copy-start.71 = (s32[1,128,8]{1,2,0:T(8,128)S(1)}, s32[1,128,8]{1,2,0:T(8,128)}, u32[]{:S(2)}) copy-start(s32[1,128,8]{1,2,0:T(8,128)} %param.22) | copy-start | bytes 12292
  14.4 12.3 %all-to-all-start = ((bf16[8,16,1024]{2,1,0:T(8,128)(2,1)}), bf16[8,16,1024]{2,1,0:T(8,128)(2,1)S(1)}, u32[]{:S(2)}, u32[]{:S(2)}) async-start(bf16[8,16,1024]{2,1,0:T(8,128)(2,1)} %copy.120), calls=%async_computation | async-start | bytes 524288 | tf_op jit(solution)/shard_map/all_to_all | solution.py:630
  19.8 101.9 %all-gather.3.cloned.1.call-start = ((), (), s32[]{:S(2)}) async-start(), calls=%async_computation.7 | async-start | bytes 6684672 | tf_op jit(solution)/shard_map/all_gather | solution.py:638
  29.8 17.6 %collective-permute-start = (bf16[128,2176]{1,0:T(8,128)(2,1)}, bf16[128,2176]{1,0:T(8,128)(2,1)}, u32[]{:S(2)}, u32[]{:S(2)}) collective-permute-start(bf16[128,2176]{1,0:T(8,128)(2,1)} %get-tuple-element.121), channel_id=1, source_target_pairs={{0,48},{16,0},{32,16},{48,32},{1,49},{17,1},{33,17},{49,33},{2,50}... | collective-permute-start | bytes 1671176 | tf_op jit(solution)/shard_map/ppermute | solution.py:570
  31.5 19.6 %collective-permute-start.2 = (bf16[128,2176]{1,0:T(8,128)(2,1)}, bf16[128,2176]{1,0:T(8,128)(2,1)}, u32[]{:S(2)}, u32[]{:S(2)}) collective-permute-start(bf16[128,2176]{1,0:T(8,128)(2,1)} %get-tuple-element.121), channel_id=1, source_target_pairs={{0,16},{16,32},{32,48},{48,0},{1,17},{17,33},{33,49},{49,1},{2,18}... | collective-permute-start | bytes 1671176 | tf_op jit(solution)/shard_map/ppermute | solution.py:571
  32.3 147.2 %copy-start.68 = (pred[128,128]{0,1:T(8,128)(4,1)}, pred[128,128]{0,1:T(8,128)(4,1)S(1)}, u32[]{:S(2)}) copy-start(pred[128,128]{0,1:T(8,128)(4,1)S(1)} %copy.122) | copy-start | bytes 49156
  32.5 147.9 %copy-start.65 = (f32[128,128]{0,1:T(8,128)}, f32[128,128]{0,1:T(8,128)S(1)}, u32[]{:S(2)}) copy-start(f32[128,128]{0,1:T(8,128)S(1)} %fusion.30) | copy-start | bytes 196612
  36.8 76.9 %all-to-all-start.1 = ((bf16[128,8,2048]{2,1,0:T(8,128)(2,1)}), bf16[128,8,2048]{2,1,0:T(8,128)(2,1)}, u32[]{:S(2)}, u32[]{:S(2)}) async-start(bf16[128,8,2048]{2,1,0:T(8,128)(2,1)} %convert_bitcast_fusion), calls=%async_computation.1 | async-start | bytes 8388608 | tf_op jit(solution)/shard_map/all_to_all | solution.py:673
  48.4 46.1 %collective-permute-start.1 = (bf16[64,2176]{1,0:T(8,128)(2,1)S(1)}, bf16[64,2176]{1,0:T(8,128)(2,1)S(1)}, u32[]{:S(2)}, u32[]{:S(2)}) collective-permute-start(bf16[64,2176]{1,0:T(8,128)(2,1)S(1)} %slice.263), channel_id=1, source_target_pairs={{0,48},{16,0},{32,16},{48,32},{1,49},{17,1},{33,17},{49,33},{2,50}... | collective-permute-start | bytes 835592 | tf_op jit(solution)/shard_map/ppermute | solution.py:572
  52.2 43.0 %collective-permute-start.3 = (bf16[64,2176]{1,0:T(8,128)(2,1)S(1)}, bf16[64,2176]{1,0:T(8,128)(2,1)S(1)}, u32[]{:S(2)}, u32[]{:S(2)}) collective-permute-start(bf16[64,2176]{1,0:T(8,128)(2,1)S(1)} %slice.264), channel_id=1, source_target_pairs={{0,16},{16,32},{32,48},{48,0},{1,17},{17,33},{33,49},{49,1},{2,18}... | collective-permute-start | bytes 835592 | tf_op jit(solution)/shard_map/ppermute | solution.py:573
  97.8 5.1 collective-permute-start.4
  126.4 13.0 %copy-start.55 = (f32[128]{0:T(128)}, f32[128]{0:T(128)S(1)}, u32[]{:S(2)}) copy-start(f32[128]{0:T(128)S(1)} %slice_reduce_fusion.5) | copy-start | bytes 1540
  126.6 12.8 %copy-start.57 = (f32[128]{0:T(128)}, f32[128]{0:T(128)S(1)}, u32[]{:S(2)}) copy-start(f32[128]{0:T(128)S(1)} %slice_reduce_fusion.4) | copy-start | bytes 1540
  139.4 11.4 %copy-start.7 = (f32[2,512,768]{2,1,0:T(8,128)}, f32[2,512,768]{2,1,0:T(8,128)S(1)}, u32[]{:S(2)}) copy-start(f32[2,512,768]{2,1,0:T(8,128)S(1)} %get-tuple-element.73.raw_ref) | copy-start | bytes 9437188
  156.9 4.2 collective-permute-start.5
  163.0 11.3 %collective-permute-start.6 = (bf16[64,2048]{1,0:T(8,128)(2,1)S(1)}, bf16[64,2048]{1,0:T(8,128)(2,1)S(1)}, u32[]{:S(2)}, u32[]{:S(2)}) collective-permute-start(bf16[64,2048]{1,0:T(8,128)(2,1)S(1)} %get-tuple-element.126), channel_id=1, source_target_pairs={{0,16},{16,32},{32,48},{48,0},{1,17},{17,33},{33,49},{49,1},{2,18}... | collective-permute-start | bytes 786440 | tf_op jit(solution)/shard_map/ppermute | solution.py:584
  166.2 9.4 %collective-permute-start.8 = (bf16[64,2048]{1,0:T(8,128)(2,1)S(1)}, bf16[64,2048]{1,0:T(8,128)(2,1)S(1)}, u32[]{:S(2)}, u32[]{:S(2)}) collective-permute-start(bf16[64,2048]{1,0:T(8,128)(2,1)S(1)} %get-tuple-element.125), channel_id=1, source_target_pairs={{0,48},{16,0},{32,16},{48,32},{1,49},{17,1},{33,17},{49,33},{2,50}... | collective-permute-start | bytes 786440 | tf_op jit(solution)/shard_map/ppermute | solution.py:585
  175.2 15.1 %collective-permute-start.7 = (bf16[128,2048]{1,0:T(8,128)(2,1)}, bf16[128,2048]{1,0:T(8,128)(2,1)}, u32[]{:S(2)}, u32[]{:S(2)}) collective-permute-start(bf16[128,2048]{1,0:T(8,128)(2,1)} %pad_maximum_fusion.4), channel_id=1, source_target_pairs={{0,16},{16,32},{32,48},{48,0},{1,17},{17,33},{33,49},{49,1},{2,18}... | collective-permute-start | bytes 1572872 | tf_op jit(solution)/shard_map/ppermute | solution.py:588
  176.5 14.0 %collective-permute-start.9 = (bf16[128,2048]{1,0:T(8,128)(2,1)}, bf16[128,2048]{1,0:T(8,128)(2,1)}, u32[]{:S(2)}, u32[]{:S(2)}) collective-permute-start(bf16[128,2048]{1,0:T(8,128)(2,1)} %pad_maximum_fusion.5), channel_id=1, source_target_pairs={{0,48},{16,0},{32,16},{48,32},{1,49},{17,1},{33,17},{49,33},{2,50}... | collective-permute-start | bytes 1572872 | tf_op jit(solution)/shard_map/ppermute | solution.py:588
  187.1 11.1 %copy-start.18 = (bf16[2048,128]{1,0:T(8,128)(2,1)}, bf16[2048,128]{1,0:T(8,128)(2,1)S(1)}, u32[]{:S(2)}) copy-start(bf16[2048,128]{1,0:T(8,128)(2,1)S(1)} %slice.288.router_ref) | copy-start | bytes 1572868
  202.1 65.7 %all-to-all-start.2 = ((bf16[128,8,2176]{2,1,0:T(8,128)(2,1)}), bf16[128,8,2176]{2,1,0:T(8,128)(2,1)}, u32[]{:S(2)}, u32[]{:S(2)}) async-start(bf16[128,8,2176]{2,1,0:T(8,128)(2,1)} %bitcast.126), calls=%async_computation.2 | async-start | bytes 8912896 | tf_op jit(solution)/shard_map/all_to_all | solution.py:695
  287.8 66.1 %copy-start.40 = (bf16[1024,768]{1,0:T(8,128)(2,1)}, bf16[1024,768]{1,0:T(8,128)(2,1)S(1)}, u32[]{:S(2)}) copy-start(bf16[1024,768]{1,0:T(8,128)(2,1)S(1)} %get-tuple-element.105.h_ref) | copy-start | bytes 4718596
  287.8 66.1 %copy-start.19 = (bf16[2048,128]{1,0:T(8,128)(2,1)S(1)}, bf16[2048,128]{1,0:T(8,128)(2,1)}, u32[]{:S(2)}) copy-start(bf16[2048,128]{1,0:T(8,128)(2,1)} %copy-done.18) | copy-start | bytes 1572868
  287.8 66.1 %copy-start.29 = (f32[128,2048]{1,0:T(8,128)S(1)}, f32[128,2048]{1,0:T(8,128)}, u32[]{:S(2)}) copy-start(f32[128,2048]{1,0:T(8,128)} %copy-done.28) | copy-start | bytes 3145732
  287.8 66.1 %copy-start.37 = (bf16[1,128,2048]{2,1,0:T(8,128)(2,1)S(1)}, bf16[1,128,2048]{2,1,0:T(8,128)(2,1)}, u32[]{:S(2)}) copy-start(bf16[1,128,2048]{2,1,0:T(8,128)(2,1)} %param.35) | copy-start | bytes 1572868
  287.8 66.1 %copy-start.50 = (bf16[128,2048]{1,0:T(8,128)(2,1)S(1)}, bf16[128,2048]{1,0:T(8,128)(2,1)}, u32[]{:S(2)}) copy-start(bf16[128,2048]{1,0:T(8,128)(2,1)} %copy-done.49) | copy-start | bytes 1572868
  356.8 13.7 %collective-permute-start.10 = (bf16[128,2048]{1,0:T(8,128)(2,1)S(1)}, bf16[128,2048]{1,0:T(8,128)(2,1)S(1)}, u32[]{:S(2)}, u32[]{:S(2)}) collective-permute-start(bf16[128,2048]{1,0:T(8,128)(2,1)S(1)} %get-tuple-element.82), channel_id=1, source_target_pairs={{0,48},{16,0},{32,16},{48,32},{1,49},{17,1},{33,17},{49,33},{2,50}... | collective-permute-start | bytes 1572872 | tf_op jit(solution)/shard_map/ppermute | solution.py:570
  357.3 14.9 %collective-permute-start.12 = (bf16[128,2048]{1,0:T(8,128)(2,1)S(1)}, bf16[128,2048]{1,0:T(8,128)(2,1)S(1)}, u32[]{:S(2)}, u32[]{:S(2)}) collective-permute-start(bf16[128,2048]{1,0:T(8,128)(2,1)S(1)} %get-tuple-element.82), channel_id=1, source_target_pairs={{0,16},{16,32},{32,48},{48,0},{1,17},{17,33},{33,49},{49,1},{2,18}... | collective-permute-start | bytes 1572872 | tf_op jit(solution)/shard_map/ppermute | solution.py:571
  370.5 14.2 %copy-start.32 = (bf16[2,512,512]{2,1,0:T(8,128)(2,1)S(1)}, bf16[2,512,512]{2,1,0:T(8,128)(2,1)}, u32[]{:S(2)}) copy-start(bf16[2,512,512]{2,1,0:T(8,128)(2,1)} %copy-done.31) | copy-start | bytes 3145732
  370.5 7.2 %collective-permute-start.11 = (bf16[64,2048]{1,0:T(8,128)(2,1)S(1)}, bf16[64,2048]{1,0:T(8,128)(2,1)S(1)}, u32[]{:S(2)}, u32[]{:S(2)}) collective-permute-start(bf16[64,2048]{1,0:T(8,128)(2,1)S(1)} %slice.289), channel_id=1, source_target_pairs={{0,48},{16,0},{32,16},{48,32},{1,49},{17,1},{33,17},{49,33},{2,50}... | collective-permute-start | bytes 786440 | tf_op jit(solution)/shard_map/ppermute | solution.py:572
  372.3 8.1 %collective-permute-start.13 = (bf16[64,2048]{1,0:T(8,128)(2,1)S(1)}, bf16[64,2048]{1,0:T(8,128)(2,1)S(1)}, u32[]{:S(2)}, u32[]{:S(2)}) collective-permute-start(bf16[64,2048]{1,0:T(8,128)(2,1)S(1)} %slice.290), channel_id=1, source_target_pairs={{0,16},{16,32},{32,48},{48,0},{1,17},{17,33},{33,49},{49,1},{2,18}... | collective-permute-start | bytes 786440 | tf_op jit(solution)/shard_map/ppermute | solution.py:573
  380.4 4.2 collective-permute-start.14
  422.0 67.0 %all-to-all-start.4 = ((bf16[128,8,2048]{2,1,0:T(8,128)(2,1)}), bf16[128,8,2048]{2,1,0:T(8,128)(2,1)}, u32[]{:S(2)}, u32[]{:S(2)}) async-start(bf16[128,8,2048]{2,1,0:T(8,128)(2,1)} %bitcast.150), calls=%async_computation.4 | async-start | bytes 8388608 | tf_op jit(solution)/shard_map/all_to_all | solution.py:709
  444.0 10.7 %copy-start.60 = (bf16[1024,768]{1,0:T(8,128)(2,1)S(1)}, bf16[1024,768]{1,0:T(8,128)(2,1)}, u32[]{:S(2)}) copy-start(bf16[1024,768]{1,0:T(8,128)(2,1)} %copy-done.59) | copy-start | bytes 4718596
  444.0 10.7 %copy-start.61 = (bf16[1024,768]{1,0:T(8,128)(2,1)S(1)}, bf16[1024,768]{1,0:T(8,128)(2,1)}, u32[]{:S(2)}) copy-start(bf16[1024,768]{1,0:T(8,128)(2,1)} %get-tuple-element.102.du_ref) | copy-start | bytes 4718596
  453.4 32.8 %collective-permute-start.15 = (bf16[512,2048]{1,0:T(8,128)(2,1)}, bf16[512,2048]{1,0:T(8,128)(2,1)}, u32[]{:S(2)}, u32[]{:S(2)}) collective-permute-start(bf16[512,2048]{1,0:T(8,128)(2,1)} %get-tuple-element.91), channel_id=1, source_target_pairs={{0,64},{64,0},{1,65},{65,1},{2,66},{66,2},{3,67},{67,3},{4,68},{68... | collective-permute-start | bytes 6291464 | tf_op jit(solution)/shard_map/ppermute | solution.py:612
  489.1 13.3 %copy-start.41 = (bf16[1024,768]{1,0:T(8,128)(2,1)S(1)}, bf16[1024,768]{1,0:T(8,128)(2,1)}, u32[]{:S(2)}) copy-start(bf16[1024,768]{1,0:T(8,128)(2,1)} %copy-done.40) | copy-start | bytes 4718596
  489.1 83.3 %all-to-all-start.5 = ((bf16[128,16,1024]{2,1,0:T(8,128)(2,1)}), bf16[128,16,1024]{2,1,0:T(8,128)(2,1)}, u32[]{:S(2)}, u32[]{:S(2)}) async-start(bf16[128,16,1024]{2,1,0:T(8,128)(2,1)} %bitcast.123), calls=%async_computation.5 | async-start | bytes 8388608 | tf_op jit(solution)/shard_map/all_to_all | solution.py:748
  499.5 52.0 %collective-permute-start.18 = (bf16[64,2048]{1,0:T(8,128)(2,1)S(1)}, bf16[64,2048]{1,0:T(8,128)(2,1)S(1)}, u32[]{:S(2)}, u32[]{:S(2)}) collective-permute-start(bf16[64,2048]{1,0:T(8,128)(2,1)S(1)} %get-tuple-element.124), channel_id=1, source_target_pairs={{0,48},{16,0},{32,16},{48,32},{1,49},{17,1},{33,17},{49,33},{2,50}... | collective-permute-start | bytes 786440 | tf_op jit(solution)/shard_map/ppermute | solution.py:585
  511.0 42.8 %copy-start.66 = (f32[128,128]{0,1:T(8,128)S(1)}, f32[128,128]{0,1:T(8,128)}, u32[]{:S(2)}) copy-start(f32[128,128]{0,1:T(8,128)} %copy-done.65) | copy-start | bytes 196612
  511.0 42.8 %copy-start.69 = (pred[128,128]{0,1:T(8,128)(4,1)S(1)}, pred[128,128]{0,1:T(8,128)(4,1)}, u32[]{:S(2)}) copy-start(pred[128,128]{0,1:T(8,128)(4,1)} %copy-done.68) | copy-start | bytes 49156
  511.1 42.1 %collective-permute-start.16 = (bf16[64,2048]{1,0:T(8,128)(2,1)S(1)}, bf16[64,2048]{1,0:T(8,128)(2,1)S(1)}, u32[]{:S(2)}, u32[]{:S(2)}) collective-permute-start(bf16[64,2048]{1,0:T(8,128)(2,1)S(1)} %get-tuple-element.123), channel_id=1, source_target_pairs={{0,16},{16,32},{32,48},{48,0},{1,17},{17,33},{33,49},{49,1},{2,18}... | collective-permute-start | bytes 786440 | tf_op jit(solution)/shard_map/ppermute | solution.py:584
  551.6 13.6 %collective-permute-start.19 = (bf16[128,2048]{1,0:T(8,128)(2,1)S(1)}, bf16[128,2048]{1,0:T(8,128)(2,1)S(1)}, u32[]{:S(2)}, u32[]{:S(2)}) collective-permute-start(bf16[128,2048]{1,0:T(8,128)(2,1)S(1)} %pad_maximum_fusion.7), channel_id=1, source_target_pairs={{0,48},{16,0},{32,16},{48,32},{1,49},{17,1},{33,17},{49,33},{2,50}... | collective-permute-start | bytes 1572872 | tf_op jit(solution)/shard_map/ppermute | solution.py:588
  553.3 15.1 %collective-permute-start.17 = (bf16[128,2048]{1,0:T(8,128)(2,1)S(1)}, bf16[128,2048]{1,0:T(8,128)(2,1)S(1)}, u32[]{:S(2)}, u32[]{:S(2)}) collective-permute-start(bf16[128,2048]{1,0:T(8,128)(2,1)S(1)} %pad_maximum_fusion.6), channel_id=1, source_target_pairs={{0,16},{16,32},{32,48},{48,0},{1,17},{17,33},{33,49},{49,1},{2,18}... | collective-permute-start | bytes 1572872 | tf_op jit(solution)/shard_map/ppermute | solution.py:588
  556.9 11.5 %copy-start.12 = (bf16[1,128,2048]{2,1,0:T(8,128)(2,1)S(1)}, bf16[1,128,2048]{2,1,0:T(8,128)(2,1)}, u32[]{:S(2)}) copy-start(bf16[1,128,2048]{2,1,0:T(8,128)(2,1)} %param.20) | copy-start | bytes 1572868
  556.9 11.5 %copy-start.15 = (f32[512,2048]{1,0:T(8,128)S(1)}, f32[512,2048]{1,0:T(8,128)}, u32[]{:S(2)}) copy-start(f32[512,2048]{1,0:T(8,128)} %copy-done.13) | copy-start | bytes 12582916
  (51 other events, 194.8 us)
Sparse Core Ops, SparseCore 0:
  27.6 94.0 all-gather.2
